TPU v7x, 128 devices: a whole 4x4x4 slice. The times are simulated.
128 devices in a mesh: group: 2 (over y_hi), blk: 64 (over z, y_lo, x, core).
Axes of the slice: x: 4, y: 4 (y_hi: 2, y_lo: 2; y = y_hi * 2 + y_lo), z: 4, core: 2. Of those that a mesh axis runs over, the one named last changes fastest.
Arguments:
- image_features: bfloat16 [98304, 1280], P(('group', 'blk')), may hold values from -1100 to 1100
- text_features: bfloat16 [98304, 1280], P(('group', 'blk')), may hold values from -1100 to 1100
- logit_scale: float32 [1], replicated, may hold values from 30 to 400
- pair_ids: int32 [98304], P(('group', 'blk')), may hold values from 0 to 98303, as said below
Outputs:
- row_gap: float32 [98304], P(('group', 'blk'))
- col_gap: float32 [98304], P(('group', 'blk'))
Inputs may be any that keep to these rules, and one draw needn't show every extreme that they name: pair_ids is a permutation of the rows in which pair_ids[i] lies in the same aligned block of 768 rows as i.
All inputs are finite; a program needn't handle non-finite values.
Results may differ from a plain program's by a relative error of at most 0.00091.
Values may be sent and summed in bfloat16 or wider, within the bound.
A program may use at most 64 MiB of HBM per device.

v0:
```python
import jax
import jax.numpy as jnp
from jax import lax
from jax.sharding import PartitionSpec as P

SHIFTS = 4


def passed_along(value, axis, steps):
    count = lax.axis_size(axis)
    pairs = [(source, (source + steps) % count) for source in range(count)]
    return lax.ppermute(value, axis, pairs)


def unit_rows(features):
    wide = features.astype(jnp.float32)
    inverse = lax.rsqrt(jnp.mean(wide * wide, axis=-1, keepdims=True) + 1e-06)
    return (wide * inverse * features.shape[-1] ** (-0.5)).astype(jnp.bfloat16)


def merge_pair(first_top, first_total, second_top, second_total):
    top = jnp.maximum(first_top, second_top)
    return (top, first_total * jnp.exp(first_top - top) + second_total * jnp.exp(second_top - top))


def tile_stats(image_unit, block, scale):
    scores = scale * lax.dot_general(
        image_unit, block, (((1,), (1,)), ((), ())), preferred_element_type=jnp.float32
    )
    col_top = jnp.max(scores, axis=0)
    col_total = jnp.sum(jnp.exp(scores - col_top[None, :]), axis=0)
    row_top = jnp.max(scores, axis=1)
    row_total = jnp.sum(jnp.exp(scores - row_top[:, None]), axis=1)
    return (scores, (row_top, row_total), (col_top, col_total))


def per_device(image_features, text_features, logit_scale, pair_ids):
    image_unit = unit_rows(image_features)
    text_unit = unit_rows(text_features)
    scale = logit_scale[0]
    rows = image_unit.shape[0]
    local = pair_ids % rows
    matches = local[:, None] == jnp.arange(rows, dtype=jnp.int32)[None, :]
    own_block = text_unit
    other_block = text_unit
    row_state = None
    carried = None
    positive = None
    coming = None
    for shift in range(SHIFTS + 1):
        if shift < SHIFTS:
            coming = (passed_along(own_block, "blk", 1), other_block)
        other_block = passed_along(own_block, "group", 1)
        scores, row_own, own_part = tile_stats(image_unit, own_block, scale)
        if shift == 0:
            positive = jnp.sum(jnp.where(matches, scores, 0.0), axis=1)
        unused, row_other, other_part = tile_stats(image_unit, other_block, scale)
        row_pair = merge_pair(row_own[0], row_own[1], row_other[0], row_other[1])
        if row_state is None:
            row_state = row_pair
        else:
            row_state = merge_pair(row_state[0], row_state[1], row_pair[0], row_pair[1])
        current = (own_part[0], own_part[1], other_part[0], other_part[1])
        if shift > 0:
            back = passed_along((current[0], current[1], current[2], current[3]), "blk", -shift)
            own_merged = merge_pair(carried[0], carried[1], back[0], back[1])
            other_merged = merge_pair(carried[2], carried[3], back[2], back[3])
            carried = (own_merged[0], own_merged[1], other_merged[0], other_merged[1])
        else:
            carried = current
        if shift < SHIFTS:
            own_block, other_block = coming
    cross = passed_along((carried[2], carried[3]), "group", -1)
    col_top, col_total = merge_pair(carried[0], carried[1], cross[0], cross[1])
    col_positive = jnp.sum(jnp.where(matches, positive[:, None], 0.0), axis=0)
    col_gap = col_top + jnp.log(col_total) - col_positive
    row_gap = row_state[0] + jnp.log(row_state[1]) - positive
    return (row_gap, col_gap)


def solution(mesh):
    placed = (P(("group", "blk"), None), P(("group", "blk"), None), P(), P(("group", "blk")))
    return jax.shard_map(
        per_device,
        mesh=mesh,
        in_specs=placed,
        out_specs=(P(("group", "blk")), P(("group", "blk"))),
        check_vma=False,
    )
```

profile of v0, /device:TPU:1, one launch (start us, length us, event | category | flops | bytes accessed | tf_op | source)
XLA Modules:
  0.0 339.1 jit_solution(9321688710467947474)
XLA Ops:
  0.6 2.1 fusion.3
  2.8 0.0 copy-start.2
  2.8 0.5 fusion.5
  3.3 2.7 collective-permute-start.1
  6.0 21.6 %collective-permute-done.1 = bf16[768,1280]{1,0:T(8,128)(2,1)S(1)} collective-permute-done((bf16[768,1280]{1,0:T(8,128)(2,1)S(1)}, bf16[768,1280]{1,0:T(8,128)(2,1)S(1)}, u32[]{:S(2)}, u32[]{:S(2)}) %collective-permute-start.1) | collective-permute-done | bytes 1966112 | tf_op jit(solution)/shard_map/ppermute | solution.py:12
  27.6 2.5 collective-permute-start.3
  30.1 2.9 collective-permute-start
  33.0 0.5 fusion
  34.1 1.9 multiply_reduce_fusion.18
  36.0 0.1 collective-permute-start.2
  36.2 1.1 exponential_reduce_fusion.9
  37.3 0.3 select_reduce_fusion
  37.6 14.1 %collective-permute-done.3 = bf16[768,1280]{1,0:T(8,128)(2,1)S(1)} collective-permute-done((bf16[768,1280]{1,0:T(8,128)(2,1)S(1)}, bf16[768,1280]{1,0:T(8,128)(2,1)S(1)}, u32[]{:S(2)}, u32[]{:S(2)}) %collective-permute-start.3) | collective-permute-done | bytes 1966112 | tf_op jit(solution)/shard_map/ppermute | solution.py:12
  51.6 2.5 collective-permute-start.5
  54.1 1.9 multiply_reduce_fusion.14
  56.0 60.2 %collective-permute-done = bf16[768,1280]{1,0:T(8,128)(2,1)S(1)} collective-permute-done((bf16[768,1280]{1,0:T(8,128)(2,1)S(1)}, bf16[768,1280]{1,0:T(8,128)(2,1)S(1)}, u32[]{:S(2)}, u32[]{:S(2)}) %collective-permute-start) | collective-permute-done | bytes 1966112 | tf_op jit(solution)/shard_map/ppermute | solution.py:12
  116.2 1.9 multiply_reduce_fusion.16
  118.1 3.8 %collective-permute-start.4 = (bf16[768,1280]{1,0:T(8,128)(2,1)S(1)}, bf16[768,1280]{1,0:T(8,128)(2,1)S(1)}, u32[]{:S(2)}, u32[]{:S(2)}) collective-permute-start(bf16[768,1280]{1,0:T(8,128)(2,1)S(1)} %collective-permute-done.3), channel_id=1, source_target_pairs={{0,64},{64,0},{1,65},{65,1},{2,66},{66,2},{3,67},{67,3},{4,68},{68... | collective-permute-start | bytes 5898248 | tf_op jit(solution)/shard_map/ppermute | solution.py:12
  121.9 0.9 exponential_reduce_fusion.8
  122.7 0.9 exponential_reduce_fusion.4
  123.6 34.7 %collective-permute-done.2 = bf16[768,1280]{1,0:T(8,128)(2,1)S(1)} collective-permute-done((bf16[768,1280]{1,0:T(8,128)(2,1)S(1)}, bf16[768,1280]{1,0:T(8,128)(2,1)S(1)}, u32[]{:S(2)}, u32[]{:S(2)}) %collective-permute-start.2) | collective-permute-done | bytes 1966112 | tf_op jit(solution)/shard_map/ppermute | solution.py:12
  158.3 1.9 multiply_reduce_fusion.12
  160.2 7.1 %collective-permute-start.13 = (f32[768]{0:T(1024)S(1)}, f32[768]{0:T(1024)S(1)}, u32[]{:S(2)}, u32[]{:S(2)}) collective-permute-start(f32[768]{0:T(1024)S(1)} %get-tuple-element.35), channel_id=1, source_target_pairs={{0,63},{1,0},{2,1},{3,2},{4,3},{5,4},{6,5},{7,6},{8,7},{9,8},{10,9... | collective-permute-start | bytes 9224 | tf_op jit(solution)/shard_map/ppermute | solution.py:12
  167.4 0.9 exponential_reduce_fusion.3
  168.2 0.6 collective-permute-start.22
  168.8 1.9 multiply_reduce_fusion.10
  170.7 0.8 exponential_reduce_fusion.7
  171.5 0.4 collective-permute-start.6
  172.0 49.6 %collective-permute-done.4 = bf16[768,1280]{1,0:T(8,128)(2,1)S(1)} collective-permute-done((bf16[768,1280]{1,0:T(8,128)(2,1)S(1)}, bf16[768,1280]{1,0:T(8,128)(2,1)S(1)}, u32[]{:S(2)}, u32[]{:S(2)}) %collective-permute-start.4) | collective-permute-done | bytes 1966112 | tf_op jit(solution)/shard_map/ppermute | solution.py:12
  221.5 1.9 multiply_reduce_fusion.8
  223.4 0.1 collective-permute-start.14
  223.5 1.9 multiply_reduce_fusion.6
  225.4 3.8 %collective-permute-start.8 = (bf16[768,1280]{1,0:T(8,128)(2,1)S(1)}, bf16[768,1280]{1,0:T(8,128)(2,1)S(1)}, u32[]{:S(2)}, u32[]{:S(2)}) collective-permute-start(bf16[768,1280]{1,0:T(8,128)(2,1)S(1)} %collective-permute-done.7), channel_id=1, source_target_pairs={{0,64},{64,0},{1,65},{65,1},{2,66},{66,2},{3,67},{67,3},{4,68},{68... | collective-permute-start | bytes 5898248 | tf_op jit(solution)/shard_map/ppermute | solution.py:12
  229.2 0.9 exponential_reduce_fusion.2
  230.1 0.9 exponential_reduce_fusion.6
  230.9 1.9 multiply_reduce_fusion.2
  232.8 0.9 exponential_reduce_fusion.5
  233.7 30.0 %collective-permute-done.6 = bf16[768,1280]{1,0:T(8,128)(2,1)S(1)} collective-permute-done((bf16[768,1280]{1,0:T(8,128)(2,1)S(1)}, bf16[768,1280]{1,0:T(8,128)(2,1)S(1)}, u32[]{:S(2)}, u32[]{:S(2)}) %collective-permute-start.6) | collective-permute-done | bytes 1966112 | tf_op jit(solution)/shard_map/ppermute | solution.py:12
  263.7 0.0 collective-permute-start.23
  263.7 1.9 multiply_reduce_fusion.4
  265.6 0.8 exponential_reduce_fusion.1
  266.4 39.4 %collective-permute-done.8 = bf16[768,1280]{1,0:T(8,128)(2,1)S(1)} collective-permute-done((bf16[768,1280]{1,0:T(8,128)(2,1)S(1)}, bf16[768,1280]{1,0:T(8,128)(2,1)S(1)}, u32[]{:S(2)}, u32[]{:S(2)}) %collective-permute-start.8) | collective-permute-done | bytes 1966112 | tf_op jit(solution)/shard_map/ppermute | solution.py:12
  305.8 1.9 multiply_reduce_fusion
  307.7 0.9 exponential_reduce_fusion
  308.6 0.1 collective-permute-start.24
  308.7 0.1 collective-permute-start.16
  308.8 1.6 collective-permute-done.15
  310.3 6.7 %collective-permute-start.25 = (f32[768]{0:T(1024)S(1)}, f32[768]{0:T(1024)S(1)}, u32[]{:S(2)}, u32[]{:S(2)}) collective-permute-start(f32[768]{0:T(1024)S(1)} %get-tuple-element.39), channel_id=1, source_target_pairs={{0,60},{1,61},{2,62},{3,63},{4,0},{5,1},{6,2},{7,3},{8,4},{9,5},{1... | collective-permute-start | bytes 9224 | tf_op jit(solution)/shard_map/ppermute | solution.py:12
  317.0 2.6 collective-permute-start.9
  319.6 0.7 collective-permute-start.18
  320.3 3.3 collective-permute-start.10
  323.6 3.1 collective-permute-start.19
  326.7 0.0 collective-permute-done.16
  326.7 1.4 collective-permute-start.20
  328.1 0.0 collective-permute-done.18
  328.2 0.6 collective-permute-start.11
  328.7 0.0 collective-permute-done.9
  328.7 2.9 collective-permute-start.21
  331.6 2.9 collective-permute-start.26
  334.5 0.1 collective-permute-start.17
  334.6 0.6 add_subtract_fusion.1
  335.2 0.3 collective-permute-done.26
  335.5 2.9 collective-permute-done.17
  338.5 0.6 add_subtract_fusion
  (27 shorter events, 0.1 us)
Async XLA Ops:
  0.6 2.2 copy-start
  2.8 30.2 %copy-start.1 = (bf16[768,1280]{1,0:T(8,128)(2,1)S(1)}, bf16[768,1280]{1,0:T(8,128)(2,1)}, u32[]{:S(2)}) copy-start(bf16[768,1280]{1,0:T(8,128)(2,1)} %param.4) | copy-start | bytes 5898244
  2.8 31.3 %copy-start.2 = (s32[768]{0:T(1024)S(1)}, s32[768]{0:T(1024)}, u32[]{:S(2)}) copy-start(s32[768]{0:T(1024)} %param.7) | copy-start | bytes 9220
  3.3 24.2 %collective-permute-start.1 = (bf16[768,1280]{1,0:T(8,128)(2,1)S(1)}, bf16[768,1280]{1,0:T(8,128)(2,1)S(1)}, u32[]{:S(2)}, u32[]{:S(2)}) collective-permute-start(bf16[768,1280]{1,0:T(8,128)(2,1)S(1)} %fusion.5), channel_id=1, source_target_pairs={{0,1},{1,2},{2,3},{3,4},{4,5},{5,6},{6,7},{7,8},{8,9},{9,10},{10,1... | collective-permute-start | bytes 5898248 | tf_op jit(solution)/shard_map/ppermute | solution.py:12
  27.6 24.1 %collective-permute-start.3 = (bf16[768,1280]{1,0:T(8,128)(2,1)S(1)}, bf16[768,1280]{1,0:T(8,128)(2,1)S(1)}, u32[]{:S(2)}, u32[]{:S(2)}) collective-permute-start(bf16[768,1280]{1,0:T(8,128)(2,1)S(1)} %collective-permute-done.1), channel_id=1, source_target_pairs={{0,1},{1,2},{2,3},{3,4},{4,5},{5,6},{6,7},{7,8},{8,9},{9,10},{10,1... | collective-permute-start | bytes 5898248 | tf_op jit(solution)/shard_map/ppermute | solution.py:12
  30.1 86.1 %collective-permute-start = (bf16[768,1280]{1,0:T(8,128)(2,1)S(1)}, bf16[768,1280]{1,0:T(8,128)(2,1)S(1)}, u32[]{:S(2)}, u32[]{:S(2)}) collective-permute-start(bf16[768,1280]{1,0:T(8,128)(2,1)S(1)} %fusion.5), channel_id=1, source_target_pairs={{0,64},{64,0},{1,65},{65,1},{2,66},{66,2},{3,67},{67,3},{4,68},{68... | collective-permute-start | bytes 5898248 | tf_op jit(solution)/shard_map/ppermute | solution.py:12
  36.0 122.3 %collective-permute-start.2 = (bf16[768,1280]{1,0:T(8,128)(2,1)S(1)}, bf16[768,1280]{1,0:T(8,128)(2,1)S(1)}, u32[]{:S(2)}, u32[]{:S(2)}) collective-permute-start(bf16[768,1280]{1,0:T(8,128)(2,1)S(1)} %collective-permute-done.1), channel_id=1, source_target_pairs={{0,64},{64,0},{1,65},{65,1},{2,66},{66,2},{3,67},{67,3},{4,68},{68... | collective-permute-start | bytes 5898248 | tf_op jit(solution)/shard_map/ppermute | solution.py:12
  51.6 115.7 %collective-permute-start.5 = (bf16[768,1280]{1,0:T(8,128)(2,1)S(1)}, bf16[768,1280]{1,0:T(8,128)(2,1)S(1)}, u32[]{:S(2)}, u32[]{:S(2)}) collective-permute-start(bf16[768,1280]{1,0:T(8,128)(2,1)S(1)} %collective-permute-done.3), channel_id=1, source_target_pairs={{0,1},{1,2},{2,3},{3,4},{4,5},{5,6},{6,7},{7,8},{8,9},{9,10},{10,1... | collective-permute-start | bytes 5898248 | tf_op jit(solution)/shard_map/ppermute | solution.py:12
  118.1 103.4 %collective-permute-start.4 = (bf16[768,1280]{1,0:T(8,128)(2,1)S(1)}, bf16[768,1280]{1,0:T(8,128)(2,1)S(1)}, u32[]{:S(2)}, u32[]{:S(2)}) collective-permute-start(bf16[768,1280]{1,0:T(8,128)(2,1)S(1)} %collective-permute-done.3), channel_id=1, source_target_pairs={{0,64},{64,0},{1,65},{65,1},{2,66},{66,2},{3,67},{67,3},{4,68},{68... | collective-permute-start | bytes 5898248 | tf_op jit(solution)/shard_map/ppermute | solution.py:12
  160.2 148.3 %collective-permute-start.13 = (f32[768]{0:T(1024)S(1)}, f32[768]{0:T(1024)S(1)}, u32[]{:S(2)}, u32[]{:S(2)}) collective-permute-start(f32[768]{0:T(1024)S(1)} %get-tuple-element.35), channel_id=1, source_target_pairs={{0,63},{1,0},{2,1},{3,2},{4,3},{5,4},{6,5},{7,6},{8,7},{9,8},{10,9... | collective-permute-start | bytes 9224 | tf_op jit(solution)/shard_map/ppermute | solution.py:12
  167.3 58.1 %collective-permute-start.7 = (bf16[768,1280]{1,0:T(8,128)(2,1)S(1)}, bf16[768,1280]{1,0:T(8,128)(2,1)S(1)}, u32[]{:S(2)}, u32[]{:S(2)}) collective-permute-start(bf16[768,1280]{1,0:T(8,128)(2,1)S(1)} %collective-permute-done.5), channel_id=1, source_target_pairs={{0,1},{1,2},{2,3},{3,4},{4,5},{5,6},{6,7},{7,8},{8,9},{9,10},{10,1... | collective-permute-start | bytes 5898248 | tf_op jit(solution)/shard_map/ppermute | solution.py:12
  168.2 148.8 %collective-permute-start.22 = (f32[768]{0:T(1024)S(1)}, f32[768]{0:T(1024)S(1)}, u32[]{:S(2)}, u32[]{:S(2)}) collective-permute-start(f32[768]{0:T(1024)S(1)} %get-tuple-element.25), channel_id=1, source_target_pairs={{0,63},{1,0},{2,1},{3,2},{4,3},{5,4},{6,5},{7,6},{8,7},{9,8},{10,9... | collective-permute-start | bytes 9224 | tf_op jit(solution)/shard_map/ppermute | solution.py:12
  171.5 92.1 %collective-permute-start.6 = (bf16[768,1280]{1,0:T(8,128)(2,1)S(1)}, bf16[768,1280]{1,0:T(8,128)(2,1)S(1)}, u32[]{:S(2)}, u32[]{:S(2)}) collective-permute-start(bf16[768,1280]{1,0:T(8,128)(2,1)S(1)} %collective-permute-done.5), channel_id=1, source_target_pairs={{0,64},{64,0},{1,65},{65,1},{2,66},{66,2},{3,67},{67,3},{4,68},{68... | collective-permute-start | bytes 5898248 | tf_op jit(solution)/shard_map/ppermute | solution.py:12
  223.4 85.2 %collective-permute-start.14 = (f32[768]{0:T(1024)S(1)}, f32[768]{0:T(1024)S(1)}, u32[]{:S(2)}, u32[]{:S(2)}) collective-permute-start(f32[768]{0:T(1024)S(1)} %get-tuple-element.33), channel_id=1, source_target_pairs={{0,62},{1,63},{2,0},{3,1},{4,2},{5,3},{6,4},{7,5},{8,6},{9,7},{10,... | collective-permute-start | bytes 9224 | tf_op jit(solution)/shard_map/ppermute | solution.py:12
  225.4 80.3 %collective-permute-start.8 = (bf16[768,1280]{1,0:T(8,128)(2,1)S(1)}, bf16[768,1280]{1,0:T(8,128)(2,1)S(1)}, u32[]{:S(2)}, u32[]{:S(2)}) collective-permute-start(bf16[768,1280]{1,0:T(8,128)(2,1)S(1)} %collective-permute-done.7), channel_id=1, source_target_pairs={{0,64},{64,0},{1,65},{65,1},{2,66},{66,2},{3,67},{67,3},{4,68},{68... | collective-permute-start | bytes 5898248 | tf_op jit(solution)/shard_map/ppermute | solution.py:12
  263.7 55.9 %collective-permute-start.23 = (f32[768]{0:T(1024)S(1)}, f32[768]{0:T(1024)S(1)}, u32[]{:S(2)}, u32[]{:S(2)}) collective-permute-start(f32[768]{0:T(1024)S(1)} %get-tuple-element.27), channel_id=1, source_target_pairs={{0,62},{1,63},{2,0},{3,1},{4,2},{5,3},{6,4},{7,5},{8,6},{9,7},{10,... | collective-permute-start | bytes 9224 | tf_op jit(solution)/shard_map/ppermute | solution.py:12
  305.8 4.5 %collective-permute-start.15 = (f32[768]{0:T(1024)S(1)}, f32[768]{0:T(1024)S(1)}, u32[]{:S(2)}, u32[]{:S(2)}) collective-permute-start(f32[768]{0:T(1024)S(1)} %get-tuple-element.31), channel_id=1, source_target_pairs={{0,61},{1,62},{2,63},{3,0},{4,1},{5,2},{6,3},{7,4},{8,5},{9,6},{10... | collective-permute-start | bytes 9224 | tf_op jit(solution)/shard_map/ppermute | solution.py:12
  308.6 11.7 %collective-permute-start.24 = (f32[768]{0:T(1024)S(1)}, f32[768]{0:T(1024)S(1)}, u32[]{:S(2)}, u32[]{:S(2)}) collective-permute-start(f32[768]{0:T(1024)S(1)} %get-tuple-element.29), channel_id=1, source_target_pairs={{0,61},{1,62},{2,63},{3,0},{4,1},{5,2},{6,3},{7,4},{8,5},{9,6},{10... | collective-permute-start | bytes 9224 | tf_op jit(solution)/shard_map/ppermute | solution.py:12
  308.7 18.0 %collective-permute-start.16 = (f32[768]{0:T(1024)S(1)}, f32[768]{0:T(1024)S(1)}, u32[]{:S(2)}, u32[]{:S(2)}) collective-permute-start(f32[768]{0:T(1024)S(1)} %get-tuple-element.41), channel_id=1, source_target_pairs={{0,60},{1,61},{2,62},{3,63},{4,0},{5,1},{6,2},{7,3},{8,4},{9,5},{1... | collective-permute-start | bytes 9224 | tf_op jit(solution)/shard_map/ppermute | solution.py:12
  310.3 13.3 %collective-permute-start.25 = (f32[768]{0:T(1024)S(1)}, f32[768]{0:T(1024)S(1)}, u32[]{:S(2)}, u32[]{:S(2)}) collective-permute-start(f32[768]{0:T(1024)S(1)} %get-tuple-element.39), channel_id=1, source_target_pairs={{0,60},{1,61},{2,62},{3,63},{4,0},{5,1},{6,2},{7,3},{8,4},{9,5},{1... | collective-permute-start | bytes 9224 | tf_op jit(solution)/shard_map/ppermute | solution.py:12
  317.0 11.7 %collective-permute-start.9 = (f32[768]{0:T(1024)S(1)}, f32[768]{0:T(1024)S(1)}, u32[]{:S(2)}, u32[]{:S(2)}) collective-permute-start(f32[768]{0:T(1024)S(1)} %get-tuple-element.9), channel_id=1, source_target_pairs={{0,63},{1,0},{2,1},{3,2},{4,3},{5,4},{6,5},{7,6},{8,7},{9,8},{10,9... | collective-permute-start | bytes 9224 | tf_op jit(solution)/shard_map/ppermute | solution.py:12
  319.6 8.6 %collective-permute-start.18 = (f32[768]{0:T(1024)S(1)}, f32[768]{0:T(1024)S(1)}, u32[]{:S(2)}, u32[]{:S(2)}) collective-permute-start(f32[768]{0:T(1024)S(1)} %get-tuple-element.7), channel_id=1, source_target_pairs={{0,63},{1,0},{2,1},{3,2},{4,3},{5,4},{6,5},{7,6},{8,7},{9,8},{10,9... | collective-permute-start | bytes 9224 | tf_op jit(solution)/shard_map/ppermute | solution.py:12
  320.3 11.3 %collective-permute-start.10 = (f32[768]{0:T(1024)S(1)}, f32[768]{0:T(1024)S(1)}, u32[]{:S(2)}, u32[]{:S(2)}) collective-permute-start(f32[768]{0:T(1024)S(1)} %get-tuple-element.13), channel_id=1, source_target_pairs={{0,62},{1,63},{2,0},{3,1},{4,2},{5,3},{6,4},{7,5},{8,6},{9,7},{10,... | collective-permute-start | bytes 9224 | tf_op jit(solution)/shard_map/ppermute | solution.py:12
  323.6 5.1 %collective-permute-start.19 = (f32[768]{0:T(1024)S(1)}, f32[768]{0:T(1024)S(1)}, u32[]{:S(2)}, u32[]{:S(2)}) collective-permute-start(f32[768]{0:T(1024)S(1)} %get-tuple-element.11), channel_id=1, source_target_pairs={{0,62},{1,63},{2,0},{3,1},{4,2},{5,3},{6,4},{7,5},{8,6},{9,7},{10,... | collective-permute-start | bytes 9224 | tf_op jit(solution)/shard_map/ppermute | solution.py:12
  326.7 7.8 %collective-permute-start.20 = (f32[768]{0:T(1024)S(1)}, f32[768]{0:T(1024)S(1)}, u32[]{:S(2)}, u32[]{:S(2)}) collective-permute-start(f32[768]{0:T(1024)S(1)} %get-tuple-element.15), channel_id=1, source_target_pairs={{0,61},{1,62},{2,63},{3,0},{4,1},{5,2},{6,3},{7,4},{8,5},{9,6},{10... | collective-permute-start | bytes 9224 | tf_op jit(solution)/shard_map/ppermute | solution.py:12
  328.2 7.1 %collective-permute-start.11 = (f32[768]{0:T(1024)S(1)}, f32[768]{0:T(1024)S(1)}, u32[]{:S(2)}, u32[]{:S(2)}) collective-permute-start(f32[768]{0:T(1024)S(1)} %get-tuple-element.17), channel_id=1, source_target_pairs={{0,61},{1,62},{2,63},{3,0},{4,1},{5,2},{6,3},{7,4},{8,5},{9,6},{10... | collective-permute-start | bytes 9224 | tf_op jit(solution)/shard_map/ppermute | solution.py:12
  328.7 6.5 %collective-permute-start.12 = (f32[768]{0:T(1024)S(1)}, f32[768]{0:T(1024)S(1)}, u32[]{:S(2)}, u32[]{:S(2)}) collective-permute-start(f32[768]{0:T(1024)S(1)} %get-tuple-element.21), channel_id=1, source_target_pairs={{0,60},{1,61},{2,62},{3,63},{4,0},{5,1},{6,2},{7,3},{8,4},{9,5},{1... | collective-permute-start | bytes 9224 | tf_op jit(solution)/shard_map/ppermute | solution.py:12
  328.7 6.5 %collective-permute-start.21 = (f32[768]{0:T(1024)S(1)}, f32[768]{0:T(1024)S(1)}, u32[]{:S(2)}, u32[]{:S(2)}) collective-permute-start(f32[768]{0:T(1024)S(1)} %get-tuple-element.19), channel_id=1, source_target_pairs={{0,60},{1,61},{2,62},{3,63},{4,0},{5,1},{6,2},{7,3},{8,4},{9,5},{1... | collective-permute-start | bytes 9224 | tf_op jit(solution)/shard_map/ppermute | solution.py:12
  331.6 4.0 %collective-permute-start.26 = (f32[768]{0:T(1024)S(1)}, f32[768]{0:T(1024)S(1)}, u32[]{:S(2)}, u32[]{:S(2)}) collective-permute-start(f32[768]{0:T(1024)S(1)} %get-tuple-element.43), channel_id=1, source_target_pairs={{0,64},{64,0},{1,65},{65,1},{2,66},{66,2},{3,67},{67,3},{4,68},{68... | collective-permute-start | bytes 9224 | tf_op jit(solution)/shard_map/ppermute | solution.py:12
  334.5 4.0 %collective-permute-start.17 = (f32[768]{0:T(1024)S(1)}, f32[768]{0:T(1024)S(1)}, u32[]{:S(2)}, u32[]{:S(2)}) collective-permute-start(f32[768]{0:T(1024)S(1)} %get-tuple-element.44), channel_id=1, source_target_pairs={{0,64},{64,0},{1,65},{65,1},{2,66},{66,2},{3,67},{67,3},{4,68},{68... | collective-permute-start | bytes 9224 | tf_op jit(solution)/shard_map/ppermute | solution.py:12
where the time goes:
time: 343 us; the launch traced here: 339 us
  waiting for transfers between devices  254 us (74%)
  starting transfers between devices  50.8 us (15%)
  matrix products  19.1 us (6%)
  other arithmetic  13.4 us (4%)
    ppermute x27, waiting for transfers between devices, passed_along(): return lax.ppermute(value, axis, pairs)  254 us
    ppermute x27, starting transfers between devices, passed_along(): return lax.ppermute(value, axis, pairs)  50.8 us
    dot_general x10, matrix products, tile_stats(): lax.dot_general(image_unit, block, (((1,), (1,)), ((), ())), preferred_el...  19.1 us
    reduce_sum x10, other arithmetic, tile_stats(): col_total = jnp.sum(jnp.exp(scores - col_top[None, :]), axis=0)  8.74 us
  transfers between devices with their start and end apart: 27, of which 10 were waited for; matrix products, arithmetic and copies ran while one was open for 9% of the time, Pallas kernels for 0%

commit v1 on v0

v1 whole, which is shorter than its diff:
```python
import math

import jax
import jax.numpy as jnp
from jax import lax
from jax.experimental import pallas as pl
from jax.experimental.pallas import tpu as pltpu
from jax.sharding import PartitionSpec as P

MESH = pl.DeviceIdType.MESH
ROWS = 768
D = 1280
NBLK = 64
Q = 128
NQ = ROWS // Q
NA = 2
MI = 384
NT = 256
LOG2E = math.log2(math.e)
LN2 = math.log(2.0)
LOW = -1e30

K_I, K_A, K_C, K_O, K_A2, K_B, K_R, K_R2, K_R2B, K_B2 = range(10)
A_I, A_A, A_A2, A_B, A_B2, A_R, A_R2 = range(7)


def kernel(img_hbm, txt_hbm, scale_ref, pair_ref, row_out, col_out,
           raw_i, raw_t, img, txt, relay, relay2, rm, rs, cm, cs, posr, posc, loc,
           stat_out, stat_in, ss, rsem, lsem, st_s, st_r):
    g = lax.axis_index("group")
    b = lax.axis_index("blk")
    j = b % 2
    x = (b // 2) % 4
    wrap3 = x // 3
    wrap2 = x // 2
    first1 = 1 - (x + 2) // 3
    first2 = 1 - x // 2

    def at(group, blk):
        return (group % 2, (blk + 2 * NBLK) % NBLK)

    row0 = b - 2 * x
    other_group = at(g + 1, b)
    other_core = at(g, b + 1 - 2 * j)
    nxt = at(g + j * wrap3, b + 2)
    nxt_from = at(g + j * first1, b - 2)
    xprev = at(g, row0 + 2 * ((x + 3) % 4))
    xprev_from = at(g, row0 + 2 * ((x + 1) % 4))
    row_next = at(g + j, b + 8)
    row_prev = at(g + j, b - 8)
    row_first = at(g, row0)
    row_last = at(g, row0 + 6)
    mate1 = at(g + (1 - j) * first1, b - 2 + 1 - 2 * j)
    mate1_from = at(g + j * wrap3, b + 2 + 1 - 2 * j)
    back2 = at(g + j * first2, b - 4)
    back2_from = at(g + j * wrap2, b + 4)
    mate2 = at(g + first2, b - 3)
    mate2_from = at(g + wrap2, b + 3)

    for q in range(NQ):
        sl = pl.ds(q * Q, Q)
        pltpu.make_async_copy(txt_hbm.at[sl], raw_t.at[sl], lsem.at[0, q]).start()
        pltpu.make_async_copy(img_hbm.at[sl], raw_i.at[sl], lsem.at[1, q]).start()

    barrier = pltpu.get_barrier_semaphore()

    def hello(dev):
        pl.semaphore_signal(barrier, inc=1, device_id=dev, device_id_type=MESH)

    hello(other_group)
    hello(other_core)
    hello(nxt_from)
    hello(xprev_from)
    hello(nxt)
    hello(mate1_from)
    hello(back2_from)

    @pl.when(x % 2 == 1)
    def _():
        hello(row_prev)

    @pl.when(x == 0)
    def _():
        hello(row_last)

    @pl.when(j == 1)
    def _():
        hello(mate2_from)

    rm[...] = jnp.full_like(rm, LOW)
    rs[...] = jnp.zeros_like(rs)
    cm[...] = jnp.full_like(cm, LOW)
    cs[...] = jnp.zeros_like(cs)
    posr[...] = jnp.zeros_like(posr)
    posc[...] = jnp.zeros_like(posc)
    base = (g * NBLK + b) * ROWS
    ids = (pair_ref[...] - base).astype(jnp.float32)
    loc[...] = jnp.transpose(jnp.broadcast_to(ids, (128, ROWS)))

    pl.semaphore_wait(barrier, 7 + x % 2 + wrap3 + 1 - j)

    def span(slot, q):
        return pl.ds(pl.multiple_of(slot * ROWS + q * Q, Q), Q)

    def push(kind, arrival, q, src, dst, dev):
        return pltpu.make_async_remote_copy(
            src_ref=src, dst_ref=dst, send_sem=ss.at[kind, q], recv_sem=rsem.at[arrival, q],
            device_id=dev, device_id_type=MESH)

    def arrived(arrival, q, dst):
        push(K_I, arrival, q, dst, dst, other_core).wait_recv()

    def c_i(q):
        return push(K_I, A_I, q, img.at[span(0, q)], img.at[span(1, q)], other_group)

    def c_a(q):
        return push(K_A, A_A, q, txt.at[span(0, q)], txt.at[span(1, q)], nxt)

    def c_c(q):
        return push(K_C, A_R, q, txt.at[span(0, q)], relay.at[span(0, q)], xprev)

    def c_t(q):
        return push(K_C, A_R2, q, txt.at[span(0, q)], relay2.at[span(0, q)], row_next)

    def c_o(q):
        return push(K_O, A_B2, q, txt.at[span(0, q)], txt.at[span(4, q)], other_core)

    def c_a2(q):
        return push(K_A2, A_A2, q, txt.at[span(1, q)], txt.at[span(2, q)], other_core)

    def c_b(q):
        return push(K_B, A_B, q, txt.at[span(1, q)], txt.at[span(3, q)], nxt)

    def c_r(q):
        return push(K_R, A_B, q, relay.at[span(0, q)], txt.at[span(3, q)], xprev)

    def c_r1(q):
        return push(K_R, A_R2, q, relay.at[span(0, q)], relay2.at[span(0, q)], row_next)

    def c_d(q):
        return push(K_R2, A_B, q, relay2.at[span(0, q)], txt.at[span(3, q)], xprev)

    def c_e(q):
        return push(K_R2, A_A, q, relay2.at[span(0, q)], txt.at[span(1, q)], row_first)

    def c_f(q):
        return push(K_R2B, A_R, q, relay2.at[span(0, q)], relay.at[span(0, q)], xprev)

    def c_b2(q):
        return push(K_B2, A_B2, q, txt.at[span(3, q)], txt.at[span(4, q)], other_core)

    def unit(raw):
        wide = raw.astype(jnp.float32)
        inverse = lax.rsqrt(jnp.mean(wide * wide, axis=-1, keepdims=True) + 1e-06)
        return (wide * inverse * D ** (-0.5)).astype(jnp.bfloat16)

    def own_piece(q, carry):
        sl = span(0, q)
        pltpu.make_async_copy(txt_hbm.at[sl], raw_t.at[sl], lsem.at[0, q]).wait()
        txt[sl, :] = unit(raw_t[sl, :])

        @pl.when((x < 3) | (q < NA))
        def _():
            c_a(q).start()

        @pl.when((x < 3) & (q >= NA))
        def _():
            c_c(q).start()

        @pl.when((x == 3) & (q >= NA))
        def _():
            c_t(q).start()

        @pl.when(j == 0)
        def _():
            c_o(q).start()

        pltpu.make_async_copy(img_hbm.at[sl], raw_i.at[sl], lsem.at[1, q]).wait()
        img[sl, :] = unit(raw_i[sl, :])
        c_i(q).start()
        return carry

    lax.fori_loop(0, NQ, own_piece, 0)

    sc = scale_ref[0] * LOG2E

    def scores(ip, tp):
        return lax.dot_general(
            img[pl.ds(pl.multiple_of(ip * MI, MI), MI), :], txt[pl.ds(pl.multiple_of(tp * NT, NT), NT), :],
            (((1,), (1,)), ((), ())), preferred_element_type=jnp.float32) * sc

    def tally(ip, tp, s):
        ri = pl.ds(pl.multiple_of(ip * MI, MI), MI)
        left, right = s[:, :128], s[:, 128:]
        ro = rm[ri, :]
        rn = jnp.maximum(ro, jnp.maximum(left, right))
        rs[ri, :] = rs[ri, :] * jnp.exp2(ro - rn) + (jnp.exp2(left - rn) + jnp.exp2(right - rn))
        rm[ri, :] = rn
        s3 = s.reshape(MI // 8, 8, NT)
        co = cm[tp]
        cn = jnp.maximum(co, jnp.max(s3, axis=0))
        cs[tp] = cs[tp] * jnp.exp2(co - cn) + jnp.sum(jnp.exp2(s3 - cn[None]), axis=0)
        cm[tp] = cn

    def own_tile(n, carry):
        ip, tp = n % 2, n // 2
        s = scores(ip, tp)
        ri = pl.ds(pl.multiple_of(ip * MI, MI), MI)
        lane = lax.broadcasted_iota(jnp.int32, (MI, 128), 1).astype(jnp.float32) + (tp * NT).astype(jnp.float32)
        want = loc[ri, :]
        left = jnp.where(want == lane, s[:, :128], 0.0)
        right = jnp.where(want == lane + 128.0, s[:, 128:], 0.0)
        posr[ri, :] = posr[ri, :] + left + right
        posc[tp, :, :128] = posc[tp, :, :128] + jnp.sum(left.reshape(MI // 8, 8, 128), axis=0)
        posc[tp, :, 128:] = posc[tp, :, 128:] + jnp.sum(right.reshape(MI // 8, 8, 128), axis=0)
        tally(ip, tp, s)
        return carry

    def sweep(i0, ni, t0, nt, stride):
        def one(n, carry):
            ip, tp = i0 + n % ni, t0 + (n // ni) * stride
            tally(ip, tp, scores(ip, tp))
            return carry
        lax.fori_loop(0, ni * nt, one, 0)

    def h_i(q):
        arrived(A_I, q, img.at[span(1, q)])

    def h_a(q):
        arrived(A_A, q, txt.at[span(1, q)])
        if q < NA:
            c_b(q).start()
        c_a2(q).start()

    def h_a2(q):
        arrived(A_A2, q, txt.at[span(2, q)])

    def h_b(q):
        arrived(A_B, q, txt.at[span(3, q)])

        @pl.when(j == 1)
        def _():
            c_b2(q).start()

    def h_b2(q):
        arrived(A_B2, q, txt.at[span(4, q)])

    def h_r(q):
        arrived(A_R, q, relay.at[span(0, q)])

        @pl.when(x == 1)
        def _():
            c_r1(q).start()

        @pl.when(x != 1)
        def _():
            c_r(q).start()

    def h_r2_last(q):
        @pl.when(x == 3)
        def _():
            arrived(A_R2, q, relay2.at[span(0, q)])
            c_e(q).start()
            c_f(q).start()

    def h_r2_second(q):
        @pl.when(x == 1)
        def _():
            arrived(A_R2, q, relay2.at[span(0, q)])
            c_d(q).start()

    lax.fori_loop(0, 6, own_tile, 0)
    h_r2_last(2); h_a(0); h_r(2)
    h_r2_last(3); h_a(1); h_r(3)
    h_a2(0); h_a2(1)
    sweep(0, 2, 3, 2, 3)
    h_r2_last(4); h_a(2); h_r(4); h_r2_second(2)
    h_r2_last(5); h_a(3); h_r(5); h_r2_second(3)
    h_a2(2); h_a2(3)
    sweep(0, 2, 4, 2, 3)
    h_i(0); h_i(1); h_i(2)
    sweep(2, 1, 0, 5, 1)
    sweep(2, 1, 6, 2, 1)
    h_r2_second(4); h_r2_second(5)
    h_a(4); h_a(5); h_a2(4); h_a2(5)
    sweep(0, 3, 5, 2, 3)
    h_b(2); h_b(3); h_b2(2); h_b2(3)
    sweep(0, 3, 10, 2, 3)
    h_i(3); h_i(4); h_i(5)
    sweep(3, 1, 0, 9, 1)
    sweep(3, 1, 10, 2, 3)
    h_b(0); h_b(1); h_b2(0); h_b2(1)
    sweep(0, 4, 9, 2, 3)
    h_b(4); h_b(5); h_b2(4); h_b2(5)
    sweep(0, 4, 11, 2, 3)

    def rows_of(part):
        ri = pl.ds(part * ROWS, ROWS)
        mt = jnp.transpose(rm[ri, :])
        st = jnp.transpose(rs[ri, :])
        top = jnp.max(mt, axis=0, keepdims=True)
        return top, jnp.sum(st * jnp.exp2(mt - top), axis=0, keepdims=True)

    def cols_of(slot, u):
        m = cm[slot * 3 + u]
        top = jnp.max(m, axis=0, keepdims=True)
        return top, jnp.sum(cs[slot * 3 + u] * jnp.exp2(m - top), axis=0, keepdims=True)

    def c_stat(k, to, dev):
        return pltpu.make_async_remote_copy(
            src_ref=stat_out.at[k], dst_ref=stat_in.at[to], send_sem=st_s.at[k], recv_sem=st_r.at[to],
            device_id=dev, device_id_type=MESH)

    top, total = rows_of(1)
    stat_out[0, 0:1, :] = top
    stat_out[0, 1:2, :] = total
    c_stat(0, 0, other_group).start()
    for slot in (1, 2, 3, 4):
        for u in range(3):
            top, total = cols_of(slot, u)
            stat_out[slot, 0:1, u * NT:(u + 1) * NT] = top
            stat_out[slot, 1:2, u * NT:(u + 1) * NT] = total
    def stat_sends(act):
        act(c_stat(1, 2, nxt_from))

        @pl.when(j == 0)
        def _():
            act(c_stat(2, 1, mate1))
            act(c_stat(4, 3, mate2))

        @pl.when(j == 1)
        def _():
            act(c_stat(2, 3, mate1))
            act(c_stat(4, 1, other_core))

        act(c_stat(3, 4, back2))

    stat_sends(lambda c: c.start())

    top, total = rows_of(0)
    positive = jnp.sum(jnp.transpose(posr[...]), axis=0, keepdims=True)
    for k in range(5):
        c_stat(0, k, other_core).wait_recv()
    mine = [cols_of(0, u) for u in range(3)]
    in_top, in_total = stat_in[0, 0:1, :], stat_in[0, 1:2, :]
    m = jnp.maximum(top, in_top)
    total = total * jnp.exp2(top - m) + in_total * jnp.exp2(in_top - m)
    row_out[...] = LN2 * (m - positive) + jnp.log(total)
    for u in range(3):
        ls = slice(u * NT, (u + 1) * NT)
        top, total = mine[u]
        m = top
        for k in range(1, 5):
            m = jnp.maximum(m, stat_in[k, 0:1, ls])
        total = total * jnp.exp2(top - m)
        for k in range(1, 5):
            total = total + stat_in[k, 1:2, ls] * jnp.exp2(stat_in[k, 0:1, ls] - m)
        pc = jnp.sum(posc[u], axis=0, keepdims=True)
        col_out[:, ls] = LN2 * (m - pc) + jnp.log(total)

    c_stat(0, 0, other_group).wait_send()
    stat_sends(lambda c: c.wait_send())

    def sent(q, carry):
        c_i(q).wait_send()
        c_a2(q).wait_send()

        @pl.when((x < 3) | (q < NA))
        def _():
            c_a(q).wait_send()

        @pl.when(q < NA)
        def _():
            c_b(q).wait_send()

        @pl.when(q >= NA)
        def _():
            c_c(q).wait_send()
            c_r(q).wait_send()

        @pl.when((q >= NA) & (x % 2 == 1))
        def _():
            c_d(q).wait_send()

        @pl.when((q >= NA) & (x == 3))
        def _():
            c_f(q).wait_send()

        @pl.when(j == 0)
        def _():
            c_o(q).wait_send()

        @pl.when(j == 1)
        def _():
            c_b2(q).wait_send()

        return carry

    lax.fori_loop(0, NQ, sent, 0)


def per_device(image_features, text_features, logit_scale, pair_ids):
    vmem = pl.BlockSpec(memory_space=pltpu.VMEM)
    anywhere = pl.BlockSpec(memory_space=pl.ANY)
    smem = pl.BlockSpec(memory_space=pltpu.SMEM)
    out = jax.ShapeDtypeStruct((1, ROWS), jnp.float32)
    row_gap, col_gap = pl.pallas_call(
        kernel,
        out_shape=(out, out),
        in_specs=[anywhere, anywhere, smem, vmem],
        out_specs=(vmem, vmem),
        scratch_shapes=[
            pltpu.VMEM((ROWS, D), jnp.bfloat16),
            pltpu.VMEM((ROWS, D), jnp.bfloat16),
            pltpu.VMEM((2 * ROWS, D), jnp.bfloat16),
            pltpu.VMEM((5 * ROWS, D), jnp.bfloat16),
            pltpu.VMEM((ROWS, D), jnp.bfloat16),
            pltpu.VMEM((ROWS, D), jnp.bfloat16),
            pltpu.VMEM((2 * ROWS, 128), jnp.float32),
            pltpu.VMEM((2 * ROWS, 128), jnp.float32),
            pltpu.VMEM((15, 8, NT), jnp.float32),
            pltpu.VMEM((15, 8, NT), jnp.float32),
            pltpu.VMEM((ROWS, 128), jnp.float32),
            pltpu.VMEM((3, 8, NT), jnp.float32),
            pltpu.VMEM((ROWS, 128), jnp.float32),
            pltpu.VMEM((5, 8, ROWS), jnp.float32),
            pltpu.VMEM((5, 8, ROWS), jnp.float32),
            pltpu.SemaphoreType.DMA((10, NQ)),
            pltpu.SemaphoreType.DMA((7, NQ)),
            pltpu.SemaphoreType.DMA((2, NQ)),
            pltpu.SemaphoreType.DMA((5,)),
            pltpu.SemaphoreType.DMA((5,)),
        ],
        compiler_params=pltpu.CompilerParams(
            collective_id=0, has_side_effects=True, vmem_limit_bytes=56 * 2**20),
        cost_estimate=pl.CostEstimate(flops=15 * 10**9, bytes_accessed=4 * 10**6, transcendentals=12 * 10**6),
    )(image_features, text_features, logit_scale, pair_ids.reshape(1, ROWS))
    return (row_gap.reshape(ROWS), col_gap.reshape(ROWS))


def solution(mesh):
    placed = (P(("group", "blk"), None), P(("group", "blk"), None), P(), P(("group", "blk")))
    return jax.shard_map(
        per_device,
        mesh=mesh,
        in_specs=placed,
        out_specs=(P(("group", "blk")), P(("group", "blk"))),
        check_vma=False,
    )
```

time: 343 us -> 130 us (0.38); the launches traced: 339 us -> 130 us
  waiting for transfers between devices: 254 us -> 0 us
  Pallas kernels: 0 us -> 125 us
  starting transfers between devices: 50.8 us -> 0 us
  matrix products: 19.1 us -> 0 us
  other arithmetic: 13.4 us -> 2.56 us
    ppermute x27 -> x0, waiting for transfers between devices: 254 us -> none  [passed_along(): return lax.ppermute(value, axis, pairs)]
    pallas_call x0 -> x1, Pallas kernels: none -> 125 us  [per_device(): pl.pallas_call(kernel, out_shape=(out, out), in_specs=[anywhere, anywhere...]
    ppermute x27 -> x0, starting transfers between devices: 50.8 us -> none  [passed_along(): return lax.ppermute(value, axis, pairs)]
    dot_general x10 -> x0, matrix products: 19.1 us -> none  [tile_stats(): lax.dot_general(image_unit, block, (((1,), (1,)), ((), ())), preferred_el...]
    reduce_sum x13 -> x0, other arithmetic: 11.6 us -> none  [the longest x10 8.74 us: tile_stats(): col_total = jnp.sum(jnp.exp(scores - col_top[None, :]), axis=0)]
  transfers between devices with their start and end apart: 27 -> 0, of which waited for: 10 -> 0; matrix products, arithmetic and copies ran while one was open for 9% -> 0% of each run, Pallas kernels for 0% -> 0%
where the time goes in v1:
time: 130 us
  Pallas kernels  125 us (96%)
  other arithmetic  2.56 us (2%)
    pallas_call x1, Pallas kernels, per_device(): pl.pallas_call(kernel, out_shape=(out, out), in_specs=[anywhere, anywhere...  125 us

profile of v1, /device:TPU:1, one launch (start us, length us, event | category | flops | bytes accessed | tf_op | source)
XLA Modules:
  0.0 130.1 jit_solution(3322382814693654246)
XLA Ops:
  1.3 1.3 reshape.13.pair_ref
  2.5 125.0 %shard_map.59 = (f32[1,768]{1,0:T(1,128)}, f32[1,768]{1,0:T(1,128)}) custom-call(bf16[768,1280]{1,0:T(8,128)(2,1)} %img_hbm.1, bf16[768,1280]{1,0:T(8,128)(2,1)} %txt_hbm.1, f32[1]{0:T(128)S(6)} %copy.6.scale_ref, s32[1,768]{1,0:T(1,128)} %reshape.13.pair_ref), custom_call_target="tpu_custom_call" | custom-call | flops 15000000512 | bytes 4000000 | tf_op jit(solution)/shard_map/pallas_call | solution.py:407
  127.5 1.3 reduce
  128.8 1.3 reduce.1

commit v2 on v1

--- a/solution.py
+++ b/solution.py
@@ -11,10 +11,22 @@
 ROWS = 768
 D = 1280
 NBLK = 64
-Q = 128
+Q = 64
 NQ = ROWS // Q
-NA = 2
+NA = 4
 MI = 384
+AHEAD = 2
+SLOTS = 18
+PACE = (3, 4)
+HALF_AT, ALL_AT = 11, 17
+T_AHEAD = 3
+T_AT = 6
+LAST_AT = 1
+R0, R1, R2 = 0, 0, 3
+R_EARLY, R3 = 5, 4
+SECOND_AT = 4
+B_AT = 6
+C_B3 = 10
 NT = 256
 LOG2E = math.log2(math.e)
 LN2 = math.log(2.0)
@@ -22,6 +34,24 @@
 
 K_I, K_A, K_C, K_O, K_A2, K_B, K_R, K_R2, K_R2B, K_B2 = range(10)
 A_I, A_A, A_A2, A_B, A_B2, A_R, A_R2 = range(7)
+
+
+OWN = [(5, 3), (6, 6), (9, 4), (10, 7), (13, 5), (13, 10), (14, 8), (14, 13)]
+HALF = [(13, 20), (14, 26), (17, 21), (17, 27)]
+WIDE = [(HALF_AT, 0), (13, 2), (14, 4), (17, 1), (17, 3), (17, 5)]
+LAST = [(17, 9), (17, 11), (18, 12), (18, 14)]
+
+
+def look(values, n):
+    words = [sum(v << (6 * k) for k, v in enumerate(values[i:i + 5])) for i in range(0, len(values), 5)]
+    word = words[0]
+    for i in range(1, len(words)):
+        word = jnp.where(n // 5 == i, words[i], word)
+    return (word // (1 << (6 * (n % 5)))) % 64
+
+
+def upto(tasks):
+    return [sum(t[0] <= k for t in tasks) for k in range(SLOTS + 1)]
 
 
 def kernel(img_hbm, txt_hbm, scale_ref, pair_ref, row_out, col_out,
@@ -94,7 +124,7 @@
     posr[...] = jnp.zeros_like(posr)
     posc[...] = jnp.zeros_like(posc)
     base = (g * NBLK + b) * ROWS
-    ids = (pair_ref[...] - base).astype(jnp.float32)
+    ids = (pair_ref[...] - base).astype(jnp.float32).reshape(1, ROWS)
     loc[...] = jnp.transpose(jnp.broadcast_to(ids, (128, ROWS)))
 
     pl.semaphore_wait(barrier, 7 + x % 2 + wrap3 + 1 - j)
@@ -154,7 +184,8 @@
         inverse = lax.rsqrt(jnp.mean(wide * wide, axis=-1, keepdims=True) + 1e-06)
         return (wide * inverse * D ** (-0.5)).astype(jnp.bfloat16)
 
-    def own_piece(q, carry):
+    def own_text(n, carry):
+        q = n
         sl = span(0, q)
         pltpu.make_async_copy(txt_hbm.at[sl], raw_t.at[sl], lsem.at[0, q]).wait()
         txt[sl, :] = unit(raw_t[sl, :])
@@ -167,7 +198,7 @@
         def _():
             c_c(q).start()
 
-        @pl.when((x == 3) & (q >= NA))
+        @pl.when((x == 3) & (q >= NA) & (q < NA + T_AHEAD))
         def _():
             c_t(q).start()
 
@@ -175,124 +206,192 @@
         def _():
             c_o(q).start()
 
+        return carry
+
+    def own_image(q, carry):
+        sl = span(0, q)
         pltpu.make_async_copy(img_hbm.at[sl], raw_i.at[sl], lsem.at[1, q]).wait()
         img[sl, :] = unit(raw_i[sl, :])
-        c_i(q).start()
-        return carry
-
-    lax.fori_loop(0, NQ, own_piece, 0)
-
-    sc = scale_ref[0] * LOG2E
-
-    def scores(ip, tp):
+
+        @pl.when(q < AHEAD)
+        def _():
+            c_i(q).start()
+
+        return carry
+
+    lax.fori_loop(0, NQ, own_text, 0)
+    lax.fori_loop(0, NQ, own_image, 0)
+
+    sc = scale_ref[...].reshape(1, 1) * LOG2E
+
+    def scores(ri, tp, n=1):
         return lax.dot_general(
-            img[pl.ds(pl.multiple_of(ip * MI, MI), MI), :], txt[pl.ds(pl.multiple_of(tp * NT, NT), NT), :],
+            img[ri, :], txt[pl.ds(pl.multiple_of(tp * NT, NT), n * NT), :],
             (((1,), (1,)), ((), ())), preferred_element_type=jnp.float32) * sc
 
-    def tally(ip, tp, s):
-        ri = pl.ds(pl.multiple_of(ip * MI, MI), MI)
-        left, right = s[:, :128], s[:, 128:]
+    def tally(ri, m, tp, s):
+        n = s.shape[1] // 128
+        parts = [s[:, k * 128:(k + 1) * 128] for k in range(n)]
         ro = rm[ri, :]
-        rn = jnp.maximum(ro, jnp.maximum(left, right))
-        rs[ri, :] = rs[ri, :] * jnp.exp2(ro - rn) + (jnp.exp2(left - rn) + jnp.exp2(right - rn))
+        rn = ro
+        for part in parts:
+            rn = jnp.maximum(rn, part)
+        total = rs[ri, :] * jnp.exp2(ro - rn)
+        for part in parts:
+            total = total + jnp.exp2(part - rn)
+        rs[ri, :] = total
         rm[ri, :] = rn
-        s3 = s.reshape(MI // 8, 8, NT)
-        co = cm[tp]
-        cn = jnp.maximum(co, jnp.max(s3, axis=0))
-        cs[tp] = cs[tp] * jnp.exp2(co - cn) + jnp.sum(jnp.exp2(s3 - cn[None]), axis=0)
-        cm[tp] = cn
-
-    def own_tile(n, carry):
-        ip, tp = n % 2, n // 2
-        s = scores(ip, tp)
-        ri = pl.ds(pl.multiple_of(ip * MI, MI), MI)
-        lane = lax.broadcasted_iota(jnp.int32, (MI, 128), 1).astype(jnp.float32) + (tp * NT).astype(jnp.float32)
-        want = loc[ri, :]
+        for k in range(s.shape[1] // NT):
+            s3 = s[:, k * NT:(k + 1) * NT].reshape(m // 8, 8, NT)
+            co = cm[tp + k]
+            cn = jnp.maximum(co, jnp.max(s3, axis=0))
+            cs[tp + k] = cs[tp + k] * jnp.exp2(co - cn) + jnp.sum(jnp.exp2(s3 - cn[None]), axis=0)
+            cm[tp + k] = cn
+
+    whole = pl.ds(0, ROWS)
+
+    def pair_tile(tp, carry):
+        s = scores(whole, tp)
+        lane = (lax.broadcasted_iota(jnp.int32, (ROWS, 128), 1) + tp * NT).astype(jnp.float32)
+        want = loc[...]
         left = jnp.where(want == lane, s[:, :128], 0.0)
         right = jnp.where(want == lane + 128.0, s[:, 128:], 0.0)
-        posr[ri, :] = posr[ri, :] + left + right
-        posc[tp, :, :128] = posc[tp, :, :128] + jnp.sum(left.reshape(MI // 8, 8, 128), axis=0)
-        posc[tp, :, 128:] = posc[tp, :, 128:] + jnp.sum(right.reshape(MI // 8, 8, 128), axis=0)
-        tally(ip, tp, s)
-        return carry
-
-    def sweep(i0, ni, t0, nt, stride):
-        def one(n, carry):
-            ip, tp = i0 + n % ni, t0 + (n // ni) * stride
-            tally(ip, tp, scores(ip, tp))
-            return carry
-        lax.fori_loop(0, ni * nt, one, 0)
-
-    def h_i(q):
-        arrived(A_I, q, img.at[span(1, q)])
-
-    def h_a(q):
-        arrived(A_A, q, txt.at[span(1, q)])
-        if q < NA:
-            c_b(q).start()
-        c_a2(q).start()
-
-    def h_a2(q):
-        arrived(A_A2, q, txt.at[span(2, q)])
-
-    def h_b(q):
-        arrived(A_B, q, txt.at[span(3, q)])
-
-        @pl.when(j == 1)
-        def _():
-            c_b2(q).start()
-
-    def h_b2(q):
-        arrived(A_B2, q, txt.at[span(4, q)])
-
-    def h_r(q):
-        arrived(A_R, q, relay.at[span(0, q)])
-
-        @pl.when(x == 1)
-        def _():
-            c_r1(q).start()
-
-        @pl.when(x != 1)
-        def _():
-            c_r(q).start()
-
-    def h_r2_last(q):
-        @pl.when(x == 3)
+        posr[...] = posr[...] + left + right
+        posc[tp, :, :128] = jnp.sum(left.reshape(ROWS // 8, 8, 128), axis=0)
+        posc[tp, :, 128:] = jnp.sum(right.reshape(ROWS // 8, 8, 128), axis=0)
+        tally(whole, ROWS, tp, s)
+        return carry
+
+    def own_tile(n, carry):
+        tp = look([t[1] for t in OWN], n)
+        tally(whole, ROWS, tp, scores(whole, tp))
+        return carry
+
+    def half_tile(n, carry):
+        code = look([t[1] for t in HALF], n)
+        ri = pl.ds(pl.multiple_of(ROWS + (code % 2) * MI, MI), MI)
+        tally(ri, MI, code // 2, scores(ri, code // 2))
+        return carry
+
+    def wide_tile(n, carry):
+        code = look([t[1] for t in WIDE], n)
+        ri = pl.ds(pl.multiple_of(ROWS + (code % 2) * MI, MI), MI)
+        tp = (code // 2) * 3
+        tally(ri, MI, tp, scores(ri, tp, 3))
+        return carry
+
+    def last_tile(n, carry):
+        tp = look([t[1] for t in LAST], n)
+        both = pl.ds(0, 2 * ROWS)
+        tally(both, 2 * ROWS, tp, scores(both, tp))
+        return carry
+
+    lax.fori_loop(0, 3, pair_tile, 0)
+
+    def within(q, lo, hi):
+        return (q >= lo) & (q < hi)
+
+    def slot(t, carry):
+        q = t + T_AT
+
+        @pl.when((x == 3) & within(q, NA + T_AHEAD, NQ))
+        def _():
+            c_t(q).start()
+
+        q = t + LAST_AT
+
+        @pl.when((x == 3) & within(q, NA, NQ))
         def _():
             arrived(A_R2, q, relay2.at[span(0, q)])
             c_e(q).start()
             c_f(q).start()
 
-    def h_r2_second(q):
-        @pl.when(x == 1)
+        early = within(t + 2, NA, NA + R_EARLY)
+        q = jnp.where(x == 0, t - R0, jnp.where(x == 1, t - R1, jnp.where(x == 2, t - R2, jnp.where(early, t + 2, t - R3))))
+
+        @pl.when(within(q, NA, NQ) & ((x < 3) | early | (q >= NA + R_EARLY)))
+        def _():
+            arrived(A_R, q, relay.at[span(0, q)])
+
+            @pl.when(x == 1)
+            def _():
+                c_r1(q).start()
+
+            @pl.when(x != 1)
+            def _():
+                c_r(q).start()
+
+        q = t - 1 - first1
+
+        @pl.when(within(q, 0, NQ))
+        def _():
+            arrived(A_A, q, txt.at[span(1, q)])
+
+            @pl.when((q < NA) & (x < 3))
+            def _():
+                c_b(q).start()
+
+            c_a2(q).start()
+
+        @pl.when((x == 3) & within(t - C_B3, 0, NA))
+        def _():
+            c_b(t - C_B3).start()
+
+        q = t - SECOND_AT
+
+        @pl.when((x == 1) & within(q, NA, NQ))
         def _():
             arrived(A_R2, q, relay2.at[span(0, q)])
             c_d(q).start()
 
-    lax.fori_loop(0, 6, own_tile, 0)
-    h_r2_last(2); h_a(0); h_r(2)
-    h_r2_last(3); h_a(1); h_r(3)
-    h_a2(0); h_a2(1)
-    sweep(0, 2, 3, 2, 3)
-    h_r2_last(4); h_a(2); h_r(4); h_r2_second(2)
-    h_r2_last(5); h_a(3); h_r(5); h_r2_second(3)
-    h_a2(2); h_a2(3)
-    sweep(0, 2, 4, 2, 3)
-    h_i(0); h_i(1); h_i(2)
-    sweep(2, 1, 0, 5, 1)
-    sweep(2, 1, 6, 2, 1)
-    h_r2_second(4); h_r2_second(5)
-    h_a(4); h_a(5); h_a2(4); h_a2(5)
-    sweep(0, 3, 5, 2, 3)
-    h_b(2); h_b(3); h_b2(2); h_b2(3)
-    sweep(0, 3, 10, 2, 3)
-    h_i(3); h_i(4); h_i(5)
-    sweep(3, 1, 0, 9, 1)
-    sweep(3, 1, 10, 2, 3)
-    h_b(0); h_b(1); h_b2(0); h_b2(1)
-    sweep(0, 4, 9, 2, 3)
-    h_b(4); h_b(5); h_b2(4); h_b2(5)
-    sweep(0, 4, 11, 2, 3)
+        def second(q):
+            arrived(A_B, q, txt.at[span(3, q)])
+
+            @pl.when(j == 1)
+            def _():
+                c_b2(q).start()
+
+        @pl.when(within(t - B_AT, NA, NQ))
+        def _():
+            second(t - B_AT)
+
+        @pl.when(within(t - 14, 0, NA))
+        def _():
+            second(t - 14)
+
+        count = (t * PACE[0]) // PACE[1]
+        q = count + AHEAD - 1
+
+        @pl.when((count != ((t - 1) * PACE[0]) // PACE[1]) & within(q, AHEAD, NQ))
+        def _():
+            c_i(q).start()
+
+        @pl.when((t == HALF_AT) | (t == ALL_AT))
+        def _():
+            def image(k, carry):
+                arrived(A_I, k, img.at[span(1, k)])
+                return carry
+            half = (t // ALL_AT) * (NQ // 2)
+            lax.fori_loop(half, half + NQ // 2, image, 0)
+
+        @pl.when(within(t - 3, 0, NQ))
+        def _():
+            arrived(A_A2, t - 3, txt.at[span(2, t - 3)])
+
+        @pl.when(within(t - 7, NA, NQ))
+        def _():
+            arrived(A_B2, t - 7, txt.at[span(4, t - 7)])
+
+        @pl.when(within(t - 15, 0, NA))
+        def _():
+            arrived(A_B2, t - 15, txt.at[span(4, t - 15)])
+
+        for tasks, tile in ((OWN, own_tile), (WIDE, wide_tile), (HALF, half_tile), (LAST, last_tile)):
+            lax.fori_loop(look(upto(tasks), t - 1), look(upto(tasks), t), tile, 0)
+
+        return carry
+
+    lax.fori_loop(1, SLOTS + 1, slot, 0)
 
     def rows_of(part):
         ri = pl.ds(part * ROWS, ROWS)
@@ -345,7 +444,7 @@
     in_top, in_total = stat_in[0, 0:1, :], stat_in[0, 1:2, :]
     m = jnp.maximum(top, in_top)
     total = total * jnp.exp2(top - m) + in_total * jnp.exp2(in_top - m)
-    row_out[...] = LN2 * (m - positive) + jnp.log(total)
+    row_out[...] = (LN2 * (m - positive) + jnp.log(total)).reshape(ROWS)
     for u in range(3):
         ls = slice(u * NT, (u + 1) * NT)
         top, total = mine[u]
@@ -356,7 +455,7 @@
         for k in range(1, 5):
             total = total + stat_in[k, 1:2, ls] * jnp.exp2(stat_in[k, 0:1, ls] - m)
         pc = jnp.sum(posc[u], axis=0, keepdims=True)
-        col_out[:, ls] = LN2 * (m - pc) + jnp.log(total)
+        col_out[ls] = (LN2 * (m - pc) + jnp.log(total)).reshape(NT)
 
     c_stat(0, 0, other_group).wait_send()
     stat_sends(lambda c: c.wait_send())
@@ -402,12 +501,11 @@
 def per_device(image_features, text_features, logit_scale, pair_ids):
     vmem = pl.BlockSpec(memory_space=pltpu.VMEM)
     anywhere = pl.BlockSpec(memory_space=pl.ANY)
-    smem = pl.BlockSpec(memory_space=pltpu.SMEM)
-    out = jax.ShapeDtypeStruct((1, ROWS), jnp.float32)
-    row_gap, col_gap = pl.pallas_call(
+    out = jax.ShapeDtypeStruct((ROWS,), jnp.float32)
+    return pl.pallas_call(
         kernel,
         out_shape=(out, out),
-        in_specs=[anywhere, anywhere, smem, vmem],
+        in_specs=[anywhere, anywhere, vmem, vmem],
         out_specs=(vmem, vmem),
         scratch_shapes=[
             pltpu.VMEM((ROWS, D), jnp.bfloat16),
@@ -434,8 +532,7 @@
         compiler_params=pltpu.CompilerParams(
             collective_id=0, has_side_effects=True, vmem_limit_bytes=56 * 2**20),
         cost_estimate=pl.CostEstimate(flops=15 * 10**9, bytes_accessed=4 * 10**6, transcendentals=12 * 10**6),
-    )(image_features, text_features, logit_scale, pair_ids.reshape(1, ROWS))
-    return (row_gap.reshape(ROWS), col_gap.reshape(ROWS))
+    )(image_features, text_features, logit_scale, pair_ids)
 
 
 def solution(mesh):

time: 130 us -> 98.1 us (0.75)
  Pallas kernels: 125 us -> 94 us
  other arithmetic: 2.56 us -> 0 us
    pallas_call x1, Pallas kernels: 125 us -> 94 us  [per_device(): pl.pallas_call(kernel, out_shape=(out, out), in_specs=[anywhere, anywhere...]
    pallas_call x2 -> x0, other arithmetic: 2.56 us -> none  [per_device(): pl.pallas_call(kernel, out_shape=(out, out), in_specs=[anywhere, anywhere...]
    unnamed x0 -> x2, local copies, waits for them, and re-layouts: none -> 2.53 us
where the time goes in v2:
time: 98.1 us; the launch traced here: 97.9 us
  Pallas kernels  94 us (96%)
  local copies, waits for them, and re-layouts  2.53 us (3%)
  between operations  1.28 us (1%)
    pallas_call x1, Pallas kernels, per_device(): pl.pallas_call(kernel, out_shape=(out, out), in_specs=[anywhere, anywhere...  94 us
    unnamed x2, local copies, waits for them, and re-layouts  2.53 us

profile of v2, /device:TPU:1, one launch (start us, length us, event | category | flops | bytes accessed | tf_op | source)
XLA Modules:
  0.0 97.9 jit_solution(13989914895233407944)
XLA Ops:
  1.3 94.0 %shard_map.59 = (f32[768]{0:T(1024)}, f32[768]{0:T(1024)}) custom-call(bf16[768,1280]{1,0:T(8,128)(2,1)} %img_hbm.1, bf16[768,1280]{1,0:T(8,128)(2,1)} %txt_hbm.1, f32[1]{0:T(128)S(6)} %copy.8.scale_ref, s32[768]{0:T(1024)} %pair_ref.1), custom_call_target="tpu_custom_call" | custom-call | flops 15000000512 | bytes 4000000 | tf_op jit(solution)/shard_map/pallas_call | solution.py:505
  95.3 1.3 %copy.9 = f32[768]{0:T(1024)} copy(f32[768]{0:T(1024)} %get-tuple-element.4) | data formatting | bytes 6144
  96.6 1.3 %copy.10 = f32[768]{0:T(1024)} copy(f32[768]{0:T(1024)} %get-tuple-element.5) | data formatting | bytes 6144

commit v3 on v2

--- a/solution.py
+++ b/solution.py
@@ -13,6 +13,7 @@
 NBLK = 64
 Q = 64
 NQ = ROWS // Q
+PART = 192
 NA = 4
 MI = 384
 AHEAD = 2
@@ -37,9 +38,10 @@
 
 
 OWN = [(5, 3), (6, 6), (9, 4), (10, 7), (13, 5), (13, 10), (14, 8), (14, 13)]
-HALF = [(13, 20), (14, 26), (17, 21), (17, 27)]
-WIDE = [(HALF_AT, 0), (13, 2), (14, 4), (17, 1), (17, 3), (17, 5)]
-LAST = [(17, 9), (17, 11), (18, 12), (18, 14)]
+HALF = [(13, 20), (14, 26)]
+WIDE = [(HALF_AT, 0), (13, 2), (14, 4), (17, 3), (17, 5)]
+EARLY = [(15, 0), (16, 1)]
+LAST = [(17, 0), (18, 1)]
 
 
 def look(values, n):
@@ -54,9 +56,9 @@
     return [sum(t[0] <= k for t in tasks) for k in range(SLOTS + 1)]
 
 
-def kernel(img_hbm, txt_hbm, scale_ref, pair_ref, row_out, col_out,
-           raw_i, raw_t, img, txt, relay, relay2, rm, rs, cm, cs, posr, posc, loc,
-           stat_out, stat_in, ss, rsem, lsem, st_s, st_r):
+def kernel(img_hbm, txt_hbm, scale_hbm, pair_ref, gaps,
+           raw_i, raw_t, img, txt, relay, relay2, rm, rs, cm, cs, posr, posc, loc, posv,
+           stat_out, stat_in, ss, rsem, lsem, st_s, st_r, scale_ref, scale_sem):
     g = lax.axis_index("group")
     b = lax.axis_index("blk")
     j = b % 2
@@ -87,35 +89,44 @@
     mate2 = at(g + first2, b - 3)
     mate2_from = at(g + wrap2, b + 3)
 
-    for q in range(NQ):
-        sl = pl.ds(q * Q, Q)
-        pltpu.make_async_copy(txt_hbm.at[sl], raw_t.at[sl], lsem.at[0, q]).start()
-        pltpu.make_async_copy(img_hbm.at[sl], raw_i.at[sl], lsem.at[1, q]).start()
-
     barrier = pltpu.get_barrier_semaphore()
 
     def hello(dev):
         pl.semaphore_signal(barrier, inc=1, device_id=dev, device_id_type=MESH)
 
-    hello(other_group)
-    hello(other_core)
+    hello(nxt)
     hello(nxt_from)
-    hello(xprev_from)
-    hello(nxt)
     hello(mate1_from)
     hello(back2_from)
+
+    @pl.when(j == 1)
+    def _():
+        hello(mate2_from)
 
     @pl.when(x % 2 == 1)
     def _():
         hello(row_prev)
 
+    hello(other_group)
+    hello(xprev_from)
+
     @pl.when(x == 0)
     def _():
         hello(row_last)
 
-    @pl.when(j == 1)
-    def _():
-        hello(mate2_from)
+    hello(other_core)
+
+    get_scale = pltpu.make_async_copy(scale_hbm, scale_ref, scale_sem)
+    get_scale.start()
+
+    def fetch(kind, n):
+        sl = pl.ds(pl.multiple_of(n * PART, PART), PART)
+        src, dst = ((txt_hbm, raw_t), (img_hbm, raw_i))[kind]
+        return pltpu.make_async_copy(src.at[sl], dst.at[sl], lsem.at[kind, n])
+
+    for kind in range(2):
+        for n in range(ROWS // PART):
+            fetch(kind, n).start()
 
     rm[...] = jnp.full_like(rm, LOW)
     rs[...] = jnp.zeros_like(rs)
@@ -187,7 +198,10 @@
     def own_text(n, carry):
         q = n
         sl = span(0, q)
-        pltpu.make_async_copy(txt_hbm.at[sl], raw_t.at[sl], lsem.at[0, q]).wait()
+        @pl.when(q % (PART // Q) == 0)
+        def _():
+            fetch(0, q // (PART // Q)).wait()
+
         txt[sl, :] = unit(raw_t[sl, :])
 
         @pl.when((x < 3) | (q < NA))
@@ -210,7 +224,11 @@
 
     def own_image(q, carry):
         sl = span(0, q)
-        pltpu.make_async_copy(img_hbm.at[sl], raw_i.at[sl], lsem.at[1, q]).wait()
+
+        @pl.when(q % (PART // Q) == 0)
+        def _():
+            fetch(1, q // (PART // Q)).wait()
+
         img[sl, :] = unit(raw_i[sl, :])
 
         @pl.when(q < AHEAD)
@@ -222,14 +240,21 @@
     lax.fori_loop(0, NQ, own_text, 0)
     lax.fori_loop(0, NQ, own_image, 0)
 
-    sc = scale_ref[...].reshape(1, 1) * LOG2E
-
-    def scores(ri, tp, n=1):
+    get_scale.wait()
+    sc = scale_ref[0] * LOG2E
+
+    def mixed_text(tp, odd):
+        at0 = pl.multiple_of(tp * NT + odd * 128, 128)
+        return jnp.concatenate([txt[pl.ds(at0, 128), :], txt[pl.ds(at0 + 2 * NT, 128), :]], axis=0)
+
+    def text_of(tp):
+        return txt[pl.ds(pl.multiple_of(tp * NT, NT), NT), :]
+
+    def scores(ri, text):
         return lax.dot_general(
-            img[ri, :], txt[pl.ds(pl.multiple_of(tp * NT, NT), n * NT), :],
-            (((1,), (1,)), ((), ())), preferred_element_type=jnp.float32) * sc
-
-    def tally(ri, m, tp, s):
+            img[ri, :], text, (((1,), (1,)), ((), ())), preferred_element_type=jnp.float32) * sc
+
+    def tally(ri, m, cols, s):
         n = s.shape[1] // 128
         parts = [s[:, k * 128:(k + 1) * 128] for k in range(n)]
         ro = rm[ri, :]
@@ -241,52 +266,75 @@
             total = total + jnp.exp2(part - rn)
         rs[ri, :] = total
         rm[ri, :] = rn
-        for k in range(s.shape[1] // NT):
-            s3 = s[:, k * NT:(k + 1) * NT].reshape(m // 8, 8, NT)
-            co = cm[tp + k]
+        for k in range(n):
+            c = cols(k)
+            s3 = parts[k].reshape(m // 8, 8, 128)
+            co = cm[c]
             cn = jnp.maximum(co, jnp.max(s3, axis=0))
-            cs[tp + k] = cs[tp + k] * jnp.exp2(co - cn) + jnp.sum(jnp.exp2(s3 - cn[None]), axis=0)
-            cm[tp + k] = cn
+            cs[c] = cs[c] * jnp.exp2(co - cn) + jnp.sum(jnp.exp2(s3 - cn[None]), axis=0)
+            cm[c] = cn
 
     whole = pl.ds(0, ROWS)
 
     def pair_tile(tp, carry):
-        s = scores(whole, tp)
+        s = scores(whole, text_of(tp))
         lane = (lax.broadcasted_iota(jnp.int32, (ROWS, 128), 1) + tp * NT).astype(jnp.float32)
         want = loc[...]
         left = jnp.where(want == lane, s[:, :128], 0.0)
         right = jnp.where(want == lane + 128.0, s[:, 128:], 0.0)
-        posr[...] = posr[...] + left + right
+        posr[...] = posr[...] + (left + right)
         posc[tp, :, :128] = jnp.sum(left.reshape(ROWS // 8, 8, 128), axis=0)
         posc[tp, :, 128:] = jnp.sum(right.reshape(ROWS // 8, 8, 128), axis=0)
-        tally(whole, ROWS, tp, s)
+        tally(whole, ROWS, lambda k: 2 * tp + k, s)
         return carry
 
     def own_tile(n, carry):
         tp = look([t[1] for t in OWN], n)
-        tally(whole, ROWS, tp, scores(whole, tp))
-        return carry
+        tally(whole, ROWS, lambda k: 2 * tp + k, scores(whole, text_of(tp)))
+        return carry
+
+    def chain(*items):
+        ahead = scores(items[0][0], items[0][3]())
+        for k, (ri, m, cols, _) in enumerate(items):
+            here = ahead
+            if k + 1 < len(items):
+                ahead = scores(items[k + 1][0], items[k + 1][3]())
+            tally(ri, m, cols, here)
+
+    def panel(ri, m, tp):
+        return (ri, m, lambda k: 2 * tp + k, lambda: text_of(tp))
+
+    def mixed(ri, m, slot, odd):
+        return (ri, m, lambda k: 6 * slot + odd + 4 * k, lambda: mixed_text(3 * slot, odd))
+
+    def half_rows(code):
+        return pl.ds(pl.multiple_of(ROWS + (code % 2) * MI, MI), MI)
 
     def half_tile(n, carry):
         code = look([t[1] for t in HALF], n)
-        ri = pl.ds(pl.multiple_of(ROWS + (code % 2) * MI, MI), MI)
-        tally(ri, MI, code // 2, scores(ri, code // 2))
-        return carry
+        chain(panel(half_rows(code), MI, code // 2))
+        return carry
+
+    def wide(code):
+        chain(*[panel(half_rows(code), MI, (code // 2) * 3 + u) for u in range(3)])
 
     def wide_tile(n, carry):
-        code = look([t[1] for t in WIDE], n)
-        ri = pl.ds(pl.multiple_of(ROWS + (code % 2) * MI, MI), MI)
-        tp = (code // 2) * 3
-        tally(ri, MI, tp, scores(ri, tp, 3))
+        wide(look([t[1] for t in WIDE], n))
+        return carry
+
+    most, other, final = pl.ds(0, ROWS + MI), pl.ds(ROWS, ROWS), pl.ds(ROWS + MI, MI)
+
+    def early_tile(n, carry):
+        chain(mixed(most, ROWS + MI, 3 + n, 0))
         return carry
 
     def last_tile(n, carry):
-        tp = look([t[1] for t in LAST], n)
-        both = pl.ds(0, 2 * ROWS)
-        tally(both, 2 * ROWS, tp, scores(both, tp))
+        chain(panel(final, MI, 10 + 3 * n), mixed(final, MI, 3 + n, 0),
+              mixed(whole, ROWS, 3 + n, 1), mixed(other, ROWS, 3 + n, 1))
         return carry
 
     lax.fori_loop(0, 3, pair_tile, 0)
+    posv[...] = jnp.sum(jnp.transpose(posr[...]), axis=0, keepdims=True)
 
     def within(q, lo, hi):
         return (q >= lo) & (q < hi)
@@ -386,7 +434,9 @@
         def _():
             arrived(A_B2, t - 15, txt.at[span(4, t - 15)])
 
-        for tasks, tile in ((OWN, own_tile), (WIDE, wide_tile), (HALF, half_tile), (LAST, last_tile)):
+        for tasks, tile in (
+            (OWN, own_tile), (WIDE, wide_tile), (HALF, half_tile), (EARLY, early_tile), (LAST, last_tile),
+        ):
             lax.fori_loop(look(upto(tasks), t - 1), look(upto(tasks), t), tile, 0)
 
         return carry
@@ -401,52 +451,91 @@
         return top, jnp.sum(st * jnp.exp2(mt - top), axis=0, keepdims=True)
 
     def cols_of(slot, u):
-        m = cm[slot * 3 + u]
+        m = cm[slot * 6 + u]
         top = jnp.max(m, axis=0, keepdims=True)
-        return top, jnp.sum(cs[slot * 3 + u] * jnp.exp2(m - top), axis=0, keepdims=True)
+        return top, jnp.sum(cs[slot * 6 + u] * jnp.exp2(m - top), axis=0, keepdims=True)
 
     def c_stat(k, to, dev):
         return pltpu.make_async_remote_copy(
             src_ref=stat_out.at[k], dst_ref=stat_in.at[to], send_sem=st_s.at[k], recv_sem=st_r.at[to],
             device_id=dev, device_id_type=MESH)
 
+    for slot in (1, 2, 3, 4):
+        for u in range(6):
+            top, total = cols_of(slot, u)
+            stat_out[slot, 0:1, u * 128:(u + 1) * 128] = top
+            stat_out[slot, 1:2, u * 128:(u + 1) * 128] = total
+
+    def stat_sends(act):
+        act(c_stat(1, 2, nxt_from))
+
+        @pl.when(j == 0)
+        def _():
+            act(c_stat(2, 1, mate1))
+            act(c_stat(4, 3, mate2))
+
+        @pl.when(j == 1)
+        def _():
+            act(c_stat(2, 3, mate1))
+            act(c_stat(4, 1, other_core))
+
+        act(c_stat(3, 4, back2))
+
+    stat_sends(lambda c: c.start())
+    wide(1)
     top, total = rows_of(1)
     stat_out[0, 0:1, :] = top
     stat_out[0, 1:2, :] = total
     c_stat(0, 0, other_group).start()
-    for slot in (1, 2, 3, 4):
-        for u in range(3):
-            top, total = cols_of(slot, u)
-            stat_out[slot, 0:1, u * NT:(u + 1) * NT] = top
-            stat_out[slot, 1:2, u * NT:(u + 1) * NT] = total
-    def stat_sends(act):
-        act(c_stat(1, 2, nxt_from))
+
+    own_top, own_total = rows_of(0)
+    mine = [cols_of(0, u) for u in range(6)]
+    positive = posv[...]
+    def sent(q, carry):
+        c_i(q).wait_send()
+        c_a2(q).wait_send()
+
+        @pl.when((x < 3) | (q < NA))
+        def _():
+            c_a(q).wait_send()
+
+        @pl.when(q < NA)
+        def _():
+            c_b(q).wait_send()
+
+        @pl.when(q >= NA)
+        def _():
+            c_c(q).wait_send()
+            c_r(q).wait_send()
+
+        @pl.when((q >= NA) & (x % 2 == 1))
+        def _():
+            c_d(q).wait_send()
+
+        @pl.when((q >= NA) & (x == 3))
+        def _():
+            c_f(q).wait_send()
 
         @pl.when(j == 0)
         def _():
-            act(c_stat(2, 1, mate1))
-            act(c_stat(4, 3, mate2))
+            c_o(q).wait_send()
 
         @pl.when(j == 1)
         def _():
-            act(c_stat(2, 3, mate1))
-            act(c_stat(4, 1, other_core))
-
-        act(c_stat(3, 4, back2))
-
-    stat_sends(lambda c: c.start())
-
-    top, total = rows_of(0)
-    positive = jnp.sum(jnp.transpose(posr[...]), axis=0, keepdims=True)
+            c_b2(q).wait_send()
+
+        return carry
+
+    lax.fori_loop(0, NQ, sent, 0)
+
     for k in range(5):
         c_stat(0, k, other_core).wait_recv()
-    mine = [cols_of(0, u) for u in range(3)]
     in_top, in_total = stat_in[0, 0:1, :], stat_in[0, 1:2, :]
-    m = jnp.maximum(top, in_top)
-    total = total * jnp.exp2(top - m) + in_total * jnp.exp2(in_top - m)
-    row_out[...] = (LN2 * (m - positive) + jnp.log(total)).reshape(ROWS)
-    for u in range(3):
-        ls = slice(u * NT, (u + 1) * NT)
+    m = jnp.maximum(own_top, in_top)
+    total = own_total * jnp.exp2(own_top - m) + in_total * jnp.exp2(in_top - m)
+    gaps[:ROWS] = (LN2 * (m - positive) + jnp.log(total)).reshape(ROWS)
+    for u in range(6):
+        ls = slice(u * 128, (u + 1) * 128)
         top, total = mine[u]
         m = top
         for k in range(1, 5):
@@ -454,59 +543,22 @@
         total = total * jnp.exp2(top - m)
         for k in range(1, 5):
             total = total + stat_in[k, 1:2, ls] * jnp.exp2(stat_in[k, 0:1, ls] - m)
-        pc = jnp.sum(posc[u], axis=0, keepdims=True)
-        col_out[ls] = (LN2 * (m - pc) + jnp.log(total)).reshape(NT)
+        pc = jnp.sum(posc[u // 2, :, u % 2 * 128:(u % 2 + 1) * 128], axis=0, keepdims=True)
+        gaps[ROWS + u * 128:ROWS + (u + 1) * 128] = (LN2 * (m - pc) + jnp.log(total)).reshape(128)
 
     c_stat(0, 0, other_group).wait_send()
     stat_sends(lambda c: c.wait_send())
-
-    def sent(q, carry):
-        c_i(q).wait_send()
-        c_a2(q).wait_send()
-
-        @pl.when((x < 3) | (q < NA))
-        def _():
-            c_a(q).wait_send()
-
-        @pl.when(q < NA)
-        def _():
-            c_b(q).wait_send()
-
-        @pl.when(q >= NA)
-        def _():
-            c_c(q).wait_send()
-            c_r(q).wait_send()
-
-        @pl.when((q >= NA) & (x % 2 == 1))
-        def _():
-            c_d(q).wait_send()
-
-        @pl.when((q >= NA) & (x == 3))
-        def _():
-            c_f(q).wait_send()
-
-        @pl.when(j == 0)
-        def _():
-            c_o(q).wait_send()
-
-        @pl.when(j == 1)
-        def _():
-            c_b2(q).wait_send()
-
-        return carry
-
-    lax.fori_loop(0, NQ, sent, 0)
 
 
 def per_device(image_features, text_features, logit_scale, pair_ids):
     vmem = pl.BlockSpec(memory_space=pltpu.VMEM)
     anywhere = pl.BlockSpec(memory_space=pl.ANY)
-    out = jax.ShapeDtypeStruct((ROWS,), jnp.float32)
-    return pl.pallas_call(
+    out = jax.ShapeDtypeStruct((2 * ROWS,), jnp.float32)
+    both = pl.pallas_call(
         kernel,
-        out_shape=(out, out),
-        in_specs=[anywhere, anywhere, vmem, vmem],
-        out_specs=(vmem, vmem),
+        out_shape=out,
+        in_specs=[anywhere, anywhere, pl.BlockSpec(memory_space=pltpu.HBM), vmem],
+        out_specs=vmem,
         scratch_shapes=[
             pltpu.VMEM((ROWS, D), jnp.bfloat16),
             pltpu.VMEM((ROWS, D), jnp.bfloat16),
@@ -516,23 +568,27 @@
             pltpu.VMEM((ROWS, D), jnp.bfloat16),
             pltpu.VMEM((2 * ROWS, 128), jnp.float32),
             pltpu.VMEM((2 * ROWS, 128), jnp.float32),
-            pltpu.VMEM((15, 8, NT), jnp.float32),
-            pltpu.VMEM((15, 8, NT), jnp.float32),
+            pltpu.VMEM((30, 8, 128), jnp.float32),
+            pltpu.VMEM((30, 8, 128), jnp.float32),
             pltpu.VMEM((ROWS, 128), jnp.float32),
             pltpu.VMEM((3, 8, NT), jnp.float32),
             pltpu.VMEM((ROWS, 128), jnp.float32),
+            pltpu.VMEM((1, ROWS), jnp.float32),
             pltpu.VMEM((5, 8, ROWS), jnp.float32),
             pltpu.VMEM((5, 8, ROWS), jnp.float32),
             pltpu.SemaphoreType.DMA((10, NQ)),
             pltpu.SemaphoreType.DMA((7, NQ)),
-            pltpu.SemaphoreType.DMA((2, NQ)),
+            pltpu.SemaphoreType.DMA((2, ROWS // PART)),
             pltpu.SemaphoreType.DMA((5,)),
             pltpu.SemaphoreType.DMA((5,)),
+            pltpu.SMEM((1,), jnp.float32),
+            pltpu.SemaphoreType.DMA,
         ],
         compiler_params=pltpu.CompilerParams(
             collective_id=0, has_side_effects=True, vmem_limit_bytes=56 * 2**20),
         cost_estimate=pl.CostEstimate(flops=15 * 10**9, bytes_accessed=4 * 10**6, transcendentals=12 * 10**6),
     )(image_features, text_features, logit_scale, pair_ids)
+    return both[:ROWS], both[ROWS:]
 
 
 def solution(mesh):

time: 98.1 us -> 91.8 us (0.936)
  Pallas kernels: 94 us -> 89 us
  local copies, waits for them, and re-layouts: 2.53 us -> 1.35 us
    pallas_call x1, Pallas kernels: 94 us -> 89 us  [per_device(): pl.pallas_call(kernel, out_shape=out, in_specs=[anywhere, anywhere, pl.Bl...]
    unnamed x2 -> x0, local copies, waits for them, and re-layouts: 2.53 us -> none
    slice x0 -> x1, local copies, waits for them, and re-layouts: none -> 1.35 us  [per_device(): return (both[:ROWS], both[ROWS:])]
where the time goes in v3:
time: 91.8 us; the launch traced here: 91.6 us
  Pallas kernels  89 us (97%)
  local copies, waits for them, and re-layouts  1.35 us (1%)
  between operations  1.28 us (1%)
    pallas_call x1, Pallas kernels, per_device(): pl.pallas_call(kernel, out_shape=out, in_specs=[anywhere, anywhere, pl.Bl...  89 us

profile of v3, /device:TPU:1, one launch (start us, length us, event | category | flops | bytes accessed | tf_op | source)
XLA Modules:
  0.0 91.6 jit_solution(16643268436546637966)
XLA Ops:
  1.3 89.0 %shard_map.59 = f32[1536]{0:T(1024)} custom-call(bf16[768,1280]{1,0:T(8,128)(2,1)} %img_hbm.1, bf16[768,1280]{1,0:T(8,128)(2,1)} %txt_hbm.1, f32[1]{0:T(128)S(6)} %copy.6.scale_hbm, s32[768]{0:T(1024)} %pair_ref.1), custom_call_target="tpu_custom_call" | custom-call | flops 15000000512 | bytes 4000000 | tf_op jit(solution)/shard_map/pallas_call | solution.py:557
  90.2 1.3 %fusion = (f32[768]{0:T(1024)}, f32[768]{0:T(1024)}) fusion(f32[1536]{0:T(1024)} %shard_map.59), kind=kLoop, calls=%fused_computation | loop fusion | bytes 12288 | tf_op jit(solution)/shard_map/slice | solution.py:591

commit v4 on v3

--- a/solution.py
+++ b/solution.py
@@ -20,8 +20,8 @@
 SLOTS = 18
 PACE = (3, 4)
 HALF_AT, ALL_AT = 11, 17
-T_AHEAD = 3
-T_AT = 6
+T_AHEAD = 5
+T_AT = 8
 LAST_AT = 1
 R0, R1, R2 = 0, 0, 3
 R_EARLY, R3 = 5, 4
@@ -39,7 +39,7 @@
 
 OWN = [(5, 3), (6, 6), (9, 4), (10, 7), (13, 5), (13, 10), (14, 8), (14, 13)]
 HALF = [(13, 20), (14, 26)]
-WIDE = [(HALF_AT, 0), (13, 2), (14, 4), (17, 3), (17, 5)]
+WIDE = [(HALF_AT, 0), (13, 2), (14, 4)]
 EARLY = [(15, 0), (16, 1)]
 LAST = [(17, 0), (18, 1)]
 
@@ -89,6 +89,13 @@
     mate2 = at(g + first2, b - 3)
     mate2_from = at(g + wrap2, b + 3)
 
+    def fetch(kind, n):
+        sl = pl.ds(pl.multiple_of(n * PART, PART), PART)
+        src, dst = ((txt_hbm, raw_t), (img_hbm, raw_i))[kind]
+        return pltpu.make_async_copy(src.at[sl], dst.at[sl], lsem.at[kind, n])
+
+    fetch(0, 0).start()
+
     barrier = pltpu.get_barrier_semaphore()
 
     def hello(dev):
@@ -119,14 +126,111 @@
     get_scale = pltpu.make_async_copy(scale_hbm, scale_ref, scale_sem)
     get_scale.start()
 
-    def fetch(kind, n):
-        sl = pl.ds(pl.multiple_of(n * PART, PART), PART)
-        src, dst = ((txt_hbm, raw_t), (img_hbm, raw_i))[kind]
-        return pltpu.make_async_copy(src.at[sl], dst.at[sl], lsem.at[kind, n])
-
     for kind in range(2):
-        for n in range(ROWS // PART):
+        for n in range(1 - kind, ROWS // PART):
             fetch(kind, n).start()
+
+    pl.semaphore_wait(barrier, 7 + x % 2 + wrap3 + 1 - j)
+
+    def span(slot, q):
+        return pl.ds(pl.multiple_of(slot * ROWS + q * Q, Q), Q)
+
+    def push(kind, arrival, q, src, dst, dev):
+        return pltpu.make_async_remote_copy(
+            src_ref=src, dst_ref=dst, send_sem=ss.at[kind, q], recv_sem=rsem.at[arrival, q],
+            device_id=dev, device_id_type=MESH)
+
+    def arrived(arrival, q, dst):
+        push(K_I, arrival, q, dst, dst, other_core).wait_recv()
+
+    def c_i(q):
+        return push(K_I, A_I, q, img.at[span(0, q)], img.at[span(1, q)], other_group)
+
+    def c_a(q):
+        return push(K_A, A_A, q, txt.at[span(0, q)], txt.at[span(1, q)], nxt)
+
+    def c_c(q):
+        return push(K_C, A_R, q, txt.at[span(0, q)], relay.at[span(0, q)], xprev)
+
+    def c_t(q):
+        return push(K_C, A_R2, q, txt.at[span(0, q)], relay2.at[span(0, q)], row_next)
+
+    def c_o(q):
+        return push(K_O, A_B2, q, txt.at[span(0, q)], txt.at[span(4, q)], other_core)
+
+    def c_a2(q):
+        return push(K_A2, A_A2, q, txt.at[span(1, q)], txt.at[span(2, q)], other_core)
+
+    def c_b(q):
+        return push(K_B, A_B, q, txt.at[span(1, q)], txt.at[span(3, q)], nxt)
+
+    def c_r(q):
+        return push(K_R, A_B, q, relay.at[span(0, q)], txt.at[span(3, q)], xprev)
+
+    def c_r1(q):
+        return push(K_R, A_R2, q, relay.at[span(0, q)], relay2.at[span(0, q)], row_next)
+
+    def c_d(q):
+        return push(K_R2, A_B, q, relay2.at[span(0, q)], txt.at[span(3, q)], xprev)
+
+    def c_e(q):
+        return push(K_R2, A_A, q, relay2.at[span(0, q)], txt.at[span(1, q)], row_first)
+
+    def c_f(q):
+        return push(K_R2B, A_R, q, relay2.at[span(0, q)], relay.at[span(0, q)], xprev)
+
+    def c_b2(q):
+        return push(K_B2, A_B2, q, txt.at[span(3, q)], txt.at[span(4, q)], other_core)
+
+    def unit(raw):
+        wide = raw.astype(jnp.float32)
+        inverse = lax.rsqrt(jnp.mean(wide * wide, axis=-1, keepdims=True) + 1e-06)
+        return (wide * inverse * D ** (-0.5)).astype(jnp.bfloat16)
+
+    def own_text(n, carry):
+        q = n
+        sl = span(0, q)
+        @pl.when(q % (PART // Q) == 0)
+        def _():
+            fetch(0, q // (PART // Q)).wait()
+
+        txt[sl, :] = unit(raw_t[sl, :])
+
+        @pl.when((x < 3) | (q < NA))
+        def _():
+            c_a(q).start()
+
+        @pl.when((x < 3) & (q >= NA))
+        def _():
+            c_c(q).start()
+
+        @pl.when((x == 3) & (q >= NA) & (q < NA + T_AHEAD))
+        def _():
+            c_t(q).start()
+
+        @pl.when(j == 0)
+        def _():
+            c_o(q).start()
+
+        return carry
+
+    def own_image(q, carry):
+        sl = span(0, q)
+
+        @pl.when(q % (PART // Q) == 0)
+        def _():
+            fetch(1, q // (PART // Q)).wait()
+
+        img[sl, :] = unit(raw_i[sl, :])
+
+        @pl.when(q < AHEAD)
+        def _():
+            c_i(q).start()
+
+        return carry
+
+    lax.fori_loop(0, NQ, own_text, 0)
+    lax.fori_loop(0, NQ, own_image, 0)
 
     rm[...] = jnp.full_like(rm, LOW)
     rs[...] = jnp.zeros_like(rs)
@@ -137,108 +241,6 @@
     base = (g * NBLK + b) * ROWS
     ids = (pair_ref[...] - base).astype(jnp.float32).reshape(1, ROWS)
     loc[...] = jnp.transpose(jnp.broadcast_to(ids, (128, ROWS)))
-
-    pl.semaphore_wait(barrier, 7 + x % 2 + wrap3 + 1 - j)
-
-    def span(slot, q):
-        return pl.ds(pl.multiple_of(slot * ROWS + q * Q, Q), Q)
-
-    def push(kind, arrival, q, src, dst, dev):
-        return pltpu.make_async_remote_copy(
-            src_ref=src, dst_ref=dst, send_sem=ss.at[kind, q], recv_sem=rsem.at[arrival, q],
-            device_id=dev, device_id_type=MESH)
-
-    def arrived(arrival, q, dst):
-        push(K_I, arrival, q, dst, dst, other_core).wait_recv()
-
-    def c_i(q):
-        return push(K_I, A_I, q, img.at[span(0, q)], img.at[span(1, q)], other_group)
-
-    def c_a(q):
-        return push(K_A, A_A, q, txt.at[span(0, q)], txt.at[span(1, q)], nxt)
-
-    def c_c(q):
-        return push(K_C, A_R, q, txt.at[span(0, q)], relay.at[span(0, q)], xprev)
-
-    def c_t(q):
-        return push(K_C, A_R2, q, txt.at[span(0, q)], relay2.at[span(0, q)], row_next)
-
-    def c_o(q):
-        return push(K_O, A_B2, q, txt.at[span(0, q)], txt.at[span(4, q)], other_core)
-
-    def c_a2(q):
-        return push(K_A2, A_A2, q, txt.at[span(1, q)], txt.at[span(2, q)], other_core)
-
-    def c_b(q):
-        return push(K_B, A_B, q, txt.at[span(1, q)], txt.at[span(3, q)], nxt)
-
-    def c_r(q):
-        return push(K_R, A_B, q, relay.at[span(0, q)], txt.at[span(3, q)], xprev)
-
-    def c_r1(q):
-        return push(K_R, A_R2, q, relay.at[span(0, q)], relay2.at[span(0, q)], row_next)
-
-    def c_d(q):
-        return push(K_R2, A_B, q, relay2.at[span(0, q)], txt.at[span(3, q)], xprev)
-
-    def c_e(q):
-        return push(K_R2, A_A, q, relay2.at[span(0, q)], txt.at[span(1, q)], row_first)
-
-    def c_f(q):
-        return push(K_R2B, A_R, q, relay2.at[span(0, q)], relay.at[span(0, q)], xprev)
-
-    def c_b2(q):
-        return push(K_B2, A_B2, q, txt.at[span(3, q)], txt.at[span(4, q)], other_core)
-
-    def unit(raw):
-        wide = raw.astype(jnp.float32)
-        inverse = lax.rsqrt(jnp.mean(wide * wide, axis=-1, keepdims=True) + 1e-06)
-        return (wide * inverse * D ** (-0.5)).astype(jnp.bfloat16)
-
-    def own_text(n, carry):
-        q = n
-        sl = span(0, q)
-        @pl.when(q % (PART // Q) == 0)
-        def _():
-            fetch(0, q // (PART // Q)).wait()
-
-        txt[sl, :] = unit(raw_t[sl, :])
-
-        @pl.when((x < 3) | (q < NA))
-        def _():
-            c_a(q).start()
-
-        @pl.when((x < 3) & (q >= NA))
-        def _():
-            c_c(q).start()
-
-        @pl.when((x == 3) & (q >= NA) & (q < NA + T_AHEAD))
-        def _():
-            c_t(q).start()
-
-        @pl.when(j == 0)
-        def _():
-            c_o(q).start()
-
-        return carry
-
-    def own_image(q, carry):
-        sl = span(0, q)
-
-        @pl.when(q % (PART // Q) == 0)
-        def _():
-            fetch(1, q // (PART // Q)).wait()
-
-        img[sl, :] = unit(raw_i[sl, :])
-
-        @pl.when(q < AHEAD)
-        def _():
-            c_i(q).start()
-
-        return carry
-
-    lax.fori_loop(0, NQ, own_text, 0)
-    lax.fori_loop(0, NQ, own_image, 0)
 
     get_scale.wait()
     sc = scale_ref[0] * LOG2E
@@ -460,28 +462,45 @@
             src_ref=stat_out.at[k], dst_ref=stat_in.at[to], send_sem=st_s.at[k], recv_sem=st_r.at[to],
             device_id=dev, device_id_type=MESH)
 
-    for slot in (1, 2, 3, 4):
-        for u in range(6):
-            top, total = cols_of(slot, u)
-            stat_out[slot, 0:1, u * 128:(u + 1) * 128] = top
-            stat_out[slot, 1:2, u * 128:(u + 1) * 128] = total
-
-    def stat_sends(act):
+    def col_stats(slots):
+        for k in slots:
+            for u in range(6):
+                top, total = cols_of(k, u)
+                stat_out[k, 0:1, u * 128:(u + 1) * 128] = top
+                stat_out[k, 1:2, u * 128:(u + 1) * 128] = total
+
+    def far_sends(act):
+        act(c_stat(3, 4, back2))
+
+        @pl.when(j == 0)
+        def _():
+            act(c_stat(4, 3, mate2))
+
+        @pl.when(j == 1)
+        def _():
+            act(c_stat(4, 1, other_core))
+
+    def near_sends(act):
         act(c_stat(1, 2, nxt_from))
 
         @pl.when(j == 0)
         def _():
             act(c_stat(2, 1, mate1))
-            act(c_stat(4, 3, mate2))
 
         @pl.when(j == 1)
         def _():
             act(c_stat(2, 3, mate1))
-            act(c_stat(4, 1, other_core))
-
-        act(c_stat(3, 4, back2))
-
-    stat_sends(lambda c: c.start())
+
+    col_stats((3, 4))
+    far_sends(lambda c: c.start())
+
+    def wide_rest(n, carry):
+        wide(2 * n + 1)
+        return carry
+
+    lax.fori_loop(1, 3, wide_rest, 0)
+    col_stats((1, 2))
+    near_sends(lambda c: c.start())
     wide(1)
     top, total = rows_of(1)
     stat_out[0, 0:1, :] = top
@@ -547,7 +566,8 @@
         gaps[ROWS + u * 128:ROWS + (u + 1) * 128] = (LN2 * (m - pc) + jnp.log(total)).reshape(128)
 
     c_stat(0, 0, other_group).wait_send()
-    stat_sends(lambda c: c.wait_send())
+    far_sends(lambda c: c.wait_send())
+    near_sends(lambda c: c.wait_send())
 
 
 def per_device(image_features, text_features, logit_scale, pair_ids):

time: 91.8 us -> 91.4 us (level)
  no operation moved by 1% of the time
where the time goes in v4:
time: 91.4 us; the launch traced here: 91.2 us
  Pallas kernels  88.6 us (97%)
  local copies, waits for them, and re-layouts  1.35 us (1%)
  between operations  1.28 us (1%)
    pallas_call x1, Pallas kernels, per_device(): pl.pallas_call(kernel, out_shape=out, in_specs=[anywhere, anywhere, pl.Bl...  88.6 us

profile of v4, /device:TPU:1, one launch (start us, length us, event | category | flops | bytes accessed | tf_op | source)
XLA Modules:
  0.0 91.2 jit_solution(16086315587359692210)
XLA Ops:
  1.3 88.6 %shard_map.59 = f32[1536]{0:T(1024)} custom-call(bf16[768,1280]{1,0:T(8,128)(2,1)} %img_hbm.1, bf16[768,1280]{1,0:T(8,128)(2,1)} %txt_hbm.1, f32[1]{0:T(128)S(6)} %copy.6.scale_hbm, s32[768]{0:T(1024)} %pair_ref.1), custom_call_target="tpu_custom_call" | custom-call | flops 15000000512 | bytes 4000000 | tf_op jit(solution)/shard_map/pallas_call | solution.py:577
  89.9 1.3 %fusion = (f32[768]{0:T(1024)}, f32[768]{0:T(1024)}) fusion(f32[1536]{0:T(1024)} %shard_map.59), kind=kLoop, calls=%fused_computation | loop fusion | bytes 12288 | tf_op jit(solution)/shard_map/slice | solution.py:611

commit v5 on v4

--- a/solution.py
+++ b/solution.py
@@ -332,7 +332,7 @@
 
     def last_tile(n, carry):
         chain(panel(final, MI, 10 + 3 * n), mixed(final, MI, 3 + n, 0),
-              mixed(whole, ROWS, 3 + n, 1), mixed(other, ROWS, 3 + n, 1))
+              *[mixed(pl.ds(h * MI, MI), MI, 3 + n, 1) for h in range(4)])
         return carry
 
     lax.fori_loop(0, 3, pair_tile, 0)

time: 91.4 us -> 91.3 us (level)
  no operation moved by 1% of the time
where the time goes in v5:
time: 91.3 us; the launch traced here: 91.1 us
  Pallas kernels  88.5 us (97%)
  local copies, waits for them, and re-layouts  1.35 us (1%)
  between operations  1.28 us (1%)
    pallas_call x1, Pallas kernels, per_device(): pl.pallas_call(kernel, out_shape=out, in_specs=[anywhere, anywhere, pl.Bl...  88.5 us

profile of v5, /device:TPU:1, one launch (start us, length us, event | category | flops | bytes accessed | tf_op | source)
XLA Modules:
  0.0 91.1 jit_solution(7807636599482036326)
XLA Ops:
  1.3 88.5 %shard_map.59 = f32[1536]{0:T(1024)} custom-call(bf16[768,1280]{1,0:T(8,128)(2,1)} %img_hbm.1, bf16[768,1280]{1,0:T(8,128)(2,1)} %txt_hbm.1, f32[1]{0:T(128)S(6)} %copy.6.scale_hbm, s32[768]{0:T(1024)} %pair_ref.1), custom_call_target="tpu_custom_call" | custom-call | flops 15000000512 | bytes 4000000 | tf_op jit(solution)/shard_map/pallas_call | solution.py:577
  89.8 1.3 %fusion = (f32[768]{0:T(1024)}, f32[768]{0:T(1024)}) fusion(f32[1536]{0:T(1024)} %shard_map.59), kind=kLoop, calls=%fused_computation | loop fusion | bytes 12288 | tf_op jit(solution)/shard_map/slice | solution.py:611

commit v6 on v5

--- a/solution.py
+++ b/solution.py
@@ -494,11 +494,7 @@
     col_stats((3, 4))
     far_sends(lambda c: c.start())
 
-    def wide_rest(n, carry):
-        wide(2 * n + 1)
-        return carry
-
-    lax.fori_loop(1, 3, wide_rest, 0)
+    chain(*[panel(final, MI, tp) for tp in range(3, 9)])
     col_stats((1, 2))
     near_sends(lambda c: c.start())
     wide(1)

time: 91.3 us -> 91.3 us (level)
  no operation moved by 1% of the time
where the time goes in v6:
time: 91.3 us; the launch traced here: 91.1 us
  Pallas kernels  88.5 us (97%)
  local copies, waits for them, and re-layouts  1.35 us (1%)
  between operations  1.28 us (1%)
    pallas_call x1, Pallas kernels, per_device(): pl.pallas_call(kernel, out_shape=out, in_specs=[anywhere, anywhere, pl.Bl...  88.5 us

profile of v6, /device:TPU:1, one launch (start us, length us, event | category | flops | bytes accessed | tf_op | source)
XLA Modules:
  0.0 91.1 jit_solution(14247961563510236519)
XLA Ops:
  1.3 88.5 %shard_map.59 = f32[1536]{0:T(1024)} custom-call(bf16[768,1280]{1,0:T(8,128)(2,1)} %img_hbm.1, bf16[768,1280]{1,0:T(8,128)(2,1)} %txt_hbm.1, f32[1]{0:T(128)S(6)} %copy.6.scale_hbm, s32[768]{0:T(1024)} %pair_ref.1), custom_call_target="tpu_custom_call" | custom-call | flops 15000000512 | bytes 4000000 | tf_op jit(solution)/shard_map/pallas_call | solution.py:573
  89.8 1.3 %fusion = (f32[768]{0:T(1024)}, f32[768]{0:T(1024)}) fusion(f32[1536]{0:T(1024)} %shard_map.59), kind=kLoop, calls=%fused_computation | loop fusion | bytes 12288 | tf_op jit(solution)/shard_map/slice | solution.py:607
